TPU v7x, 32 devices: a whole 2x2x4 slice. The times are simulated.
32 devices in a mesh: fsdp: 8 (over z, y), dp: 4 (over x, core).
Axes of the slice: x: 2, y: 2, z: 4, core: 2. Of those that a mesh axis runs over, the one named last changes fastest.
Arguments:
- tokens: bfloat16 [32768, 768], P(('fsdp', 'dp')), may hold values from -6 to 6
- cotangent: bfloat16 [32768, 768], P(('fsdp', 'dp')), may hold values from -6 to 6
- lengths: int32 [128], P(('fsdp', 'dp')), may hold values from 65 to 256, as said below
- buckets: int32 [128], P(('fsdp', 'dp')), may hold values from 0 to 1, as said below
- qkv_weight: bfloat16 [768, 2304], P('fsdp', 'dp'), may hold values from -0.21875 to 0.21875
- query_value_bias: bfloat16 [1536], P('fsdp'), may hold values from -1.5 to 1.5
- out_weight: bfloat16 [768, 768], P('fsdp', 'dp'), may hold values from -0.21875 to 0.21875
- out_bias: bfloat16 [768], P('fsdp'), may hold values from -1.5 to 1.5
- up_weight: bfloat16 [768, 3072], P('fsdp', 'dp'), may hold values from -0.21875 to 0.21875
- up_bias: bfloat16 [3072], P('fsdp'), may hold values from -1.5 to 1.5
- down_weight: bfloat16 [3072, 768], P('fsdp', 'dp'), may hold values from -0.109375 to 0.109375
- down_bias: bfloat16 [768], P('fsdp'), may hold values from -1.5 to 1.5
- first_gain: bfloat16 [768], P('fsdp'), may hold values from 0.5 to 1.5
- first_shift: bfloat16 [768], P('fsdp'), may hold values from -1.5 to 1.5
- mix_gain: bfloat16 [768], P('fsdp'), may hold values from 0.5 to 1.5
- mix_shift: bfloat16 [768], P('fsdp'), may hold values from -1.5 to 1.5
- second_gain: bfloat16 [768], P('fsdp'), may hold values from 0.5 to 1.5
- second_shift: bfloat16 [768], P('fsdp'), may hold values from -1.5 to 1.5
- hidden_gain: bfloat16 [3072], P('fsdp'), may hold values from 0.5 to 1.5
- hidden_shift: bfloat16 [3072], P('fsdp'), may hold values from -1.5 to 1.5
- head_scale: bfloat16 [12], replicated, may hold values from 0.5 to 2
- position_table: bfloat16 [1536, 12], P('fsdp'), may hold values from -4 to 4
Outputs:
- result_tokens: bfloat16 [32768, 768], P(('fsdp', 'dp'))
- input_grad: bfloat16 [32768, 768], P(('fsdp', 'dp'))
- qkv_weight_grad: float32 [768, 2304], P('fsdp', 'dp')
- query_value_bias_grad: float32 [1536], P('fsdp')
- out_weight_grad: float32 [768, 768], P('fsdp', 'dp')
- out_bias_grad: float32 [768], P('fsdp')
- up_weight_grad: float32 [768, 3072], P('fsdp', 'dp')
- up_bias_grad: float32 [3072], P('fsdp')
- down_weight_grad: float32 [3072, 768], P('fsdp', 'dp')
- down_bias_grad: float32 [768], P('fsdp')
- first_gain_grad: float32 [768], P('fsdp')
- first_shift_grad: float32 [768], P('fsdp')
- mix_gain_grad: float32 [768], P('fsdp')
- mix_shift_grad: float32 [768], P('fsdp')
- second_gain_grad: float32 [768], P('fsdp')
- second_shift_grad: float32 [768], P('fsdp')
- hidden_gain_grad: float32 [3072], P('fsdp')
- hidden_shift_grad: float32 [3072], P('fsdp')
- head_scale_grad: float32 [12], replicated
- position_table_grad: float32 [1536, 12], P('fsdp')
Inputs may be any that keep to these rules, and one draw needn't show every extreme that they name: `lengths`: sequence s holds its image's patches first (64 if buckets[s] is 0, 225 if it is 1) and one or more text tokens after them; one sequence in every draw has all 256 slots live. `buckets`: 0 for an image of 64 patches on an 8 x 8 grid, 1 for 225 patches on a 15 x 15 grid.
All inputs are finite; a program needn't handle non-finite values.
Results may differ from a plain program's by a relative error of at most 0.015.
Values may be sent and summed in bfloat16 or wider, within the bound.
A program may use at most 256 MiB of HBM per device.

v0:
```python
import jax
import jax.numpy as jnp
from jax import lax
from jax.sharding import PartitionSpec as P

D = 768
HEADS = 12
HEAD_DIM = 64
SLOT = 256


norm_epsilon = 1e-05
masked_score = -1000000000.0


def layer_norm(values, gain, shift):
    center = values - jnp.mean(values, -1, keepdims=True)
    spread = jnp.mean(center * center, -1, keepdims=True)
    return center * lax.rsqrt(spread + norm_epsilon) * gain + shift


def toeplitz(line, count, offset):
    width = line.shape[-1]
    tiled = jnp.tile(line, (1,) * (line.ndim - 1) + (count + 1,))
    band = tiled[..., offset : offset + count * (width - 1)]
    return band.reshape(line.shape[:-1] + (count, width - 1))[..., :count]


def grid_bias(table, patches, side):
    text_line = jnp.transpose(table[: 2 * SLOT - 1])
    textual = toeplitz(text_line, SLOT, SLOT - 1)
    plane = jnp.transpose(table[2 * SLOT : 2 * SLOT + 992].reshape(31, 32, -1), (2, 0, 1))[
        :, :, :31
    ]
    columns = toeplitz(plane, side, 15)
    rowwise = toeplitz(jnp.transpose(columns, (0, 2, 3, 1)), side, 15)
    visual = jnp.transpose(rowwise, (0, 3, 1, 4, 2)).reshape(-1, patches, patches)
    visual = jnp.pad(visual, ((0, 0), (0, SLOT - patches), (0, SLOT - patches)))
    row_pos = jnp.arange(SLOT, dtype=jnp.int32)[:, None]
    col_pos = jnp.arange(SLOT, dtype=jnp.int32)[None, :]
    inside = (row_pos < patches) & (col_pos < patches)
    return jnp.where(inside[None], visual, textual)


def bias_grids(table):
    return (grid_bias(table, 64, 8), grid_bias(table, 225, 15))


def position_bias(table, buckets):
    small_grid, large_grid = bias_grids(table)
    return jnp.where((buckets == 0)[:, None, None, None], small_grid[None], large_grid[None])


def widen(value):
    return value.astype(jnp.float32)


def outer_product(left, right):
    return lax.dot_general(
        left, right, (((0,), (0,)), ((), ())), preferred_element_type=jnp.float32
    )


def inner_product(left, right):
    return lax.dot_general(
        left, right, (((1,), (1,)), ((), ())), preferred_element_type=jnp.float32
    )


def mix_norm(attended, scales, gain, shift):
    return layer_norm((attended * scales[None, None, :, None]).reshape(-1, D), gain, shift)


def hidden_norm(hidden, gain, shift):
    return layer_norm(jax.nn.gelu(hidden, approximate=False), gain, shift)


def assemble(mats, vecs):
    return (
        mats[0],
        vecs[0],
        mats[1],
        vecs[1],
        mats[2],
        vecs[2],
        mats[3],
        vecs[3],
        vecs[4],
        vecs[5],
        vecs[6],
        vecs[7],
        vecs[8],
        vecs[9],
        vecs[10],
        vecs[11],
        vecs[12],
    )


def gather_weights(pieces):
    rows = (
        lax.all_gather(pieces[0], "fsdp", axis=0, tiled=True),
        lax.all_gather(pieces[2], "fsdp", axis=0, tiled=True),
        lax.all_gather(pieces[4], "fsdp", axis=0, tiled=True),
        lax.all_gather(pieces[6], "fsdp", axis=0, tiled=True),
        lax.all_gather(pieces[1], "fsdp", axis=0, tiled=True),
        lax.all_gather(pieces[3], "fsdp", axis=0, tiled=True),
        lax.all_gather(pieces[5], "fsdp", axis=0, tiled=True),
        lax.all_gather(pieces[7], "fsdp", axis=0, tiled=True),
        lax.all_gather(pieces[8], "fsdp", axis=0, tiled=True),
        lax.all_gather(pieces[9], "fsdp", axis=0, tiled=True),
        lax.all_gather(pieces[10], "fsdp", axis=0, tiled=True),
        lax.all_gather(pieces[11], "fsdp", axis=0, tiled=True),
        lax.all_gather(pieces[12], "fsdp", axis=0, tiled=True),
        lax.all_gather(pieces[13], "fsdp", axis=0, tiled=True),
        lax.all_gather(pieces[14], "fsdp", axis=0, tiled=True),
        lax.all_gather(pieces[15], "fsdp", axis=0, tiled=True),
        lax.all_gather(pieces[16], "fsdp", axis=0, tiled=True),
    )
    mats = (
        lax.all_gather(rows[0], "dp", axis=1, tiled=True),
        lax.all_gather(rows[1], "dp", axis=1, tiled=True),
        lax.all_gather(rows[2], "dp", axis=1, tiled=True),
        lax.all_gather(rows[3], "dp", axis=1, tiled=True),
    )
    vecs = rows[4:]
    return assemble(mats, vecs)


def scatter_grads(grads):
    cols = (
        lax.psum_scatter(
            grads[0].astype(jnp.bfloat16), "dp", scatter_dimension=1, tiled=True
        ).astype(jnp.float32),
        lax.psum_scatter(
            grads[2].astype(jnp.bfloat16), "dp", scatter_dimension=1, tiled=True
        ).astype(jnp.float32),
        lax.psum_scatter(
            grads[4].astype(jnp.bfloat16), "dp", scatter_dimension=1, tiled=True
        ).astype(jnp.float32),
        lax.psum_scatter(
            grads[6].astype(jnp.bfloat16), "dp", scatter_dimension=1, tiled=True
        ).astype(jnp.float32),
    )
    rows = (
        lax.psum_scatter(cols[0], "fsdp", scatter_dimension=0, tiled=True),
        lax.psum_scatter(cols[1], "fsdp", scatter_dimension=0, tiled=True),
        lax.psum_scatter(cols[2], "fsdp", scatter_dimension=0, tiled=True),
        lax.psum_scatter(cols[3], "fsdp", scatter_dimension=0, tiled=True),
        lax.psum_scatter(grads[1], "fsdp", scatter_dimension=0, tiled=True),
        lax.psum_scatter(grads[3], "fsdp", scatter_dimension=0, tiled=True),
        lax.psum_scatter(grads[5], "fsdp", scatter_dimension=0, tiled=True),
        lax.psum_scatter(grads[7], "fsdp", scatter_dimension=0, tiled=True),
        lax.psum_scatter(grads[8], "fsdp", scatter_dimension=0, tiled=True),
        lax.psum_scatter(grads[9], "fsdp", scatter_dimension=0, tiled=True),
        lax.psum_scatter(grads[10], "fsdp", scatter_dimension=0, tiled=True),
        lax.psum_scatter(grads[11], "fsdp", scatter_dimension=0, tiled=True),
        lax.psum_scatter(grads[12], "fsdp", scatter_dimension=0, tiled=True),
        lax.psum_scatter(grads[13], "fsdp", scatter_dimension=0, tiled=True),
        lax.psum_scatter(grads[14], "fsdp", scatter_dimension=0, tiled=True),
        lax.psum_scatter(grads[15], "fsdp", scatter_dimension=0, tiled=True),
        lax.psum_scatter(grads[16], "fsdp", scatter_dimension=0, tiled=True),
    )
    mats = rows[:4]
    vecs = rows[4:]
    summed = lax.psum(
        (
            vecs[0],
            vecs[1],
            vecs[2],
            vecs[3],
            vecs[4],
            vecs[5],
            vecs[6],
            vecs[7],
            vecs[8],
            vecs[9],
            vecs[10],
            vecs[11],
            vecs[12],
        ),
        "dp",
    )
    return assemble(mats, summed)


def forward_pass(inputs, weights, scales, lengths, buckets):
    (
        qkv_weight,
        query_value_bias,
        out_weight,
        out_bias,
        up_weight,
        up_bias,
        down_weight,
        down_bias,
        first_gain,
        first_shift,
        mix_gain,
        mix_shift,
        second_gain,
        second_shift,
        hidden_gain,
        hidden_shift,
        position_table,
    ) = weights
    count = lengths.shape[0]
    quad = (count, SLOT, HEADS, HEAD_DIM)
    scale = HEAD_DIM ** (-0.5)
    normed = layer_norm(inputs, widen(first_gain), widen(first_shift)).astype(jnp.bfloat16)
    bias_pair = widen(query_value_bias)
    zeros = jnp.zeros((D,), jnp.float32)
    projected = jnp.dot(normed, qkv_weight, preferred_element_type=jnp.float32) + jnp.concatenate(
        [bias_pair[:D], zeros, bias_pair[D:]]
    )
    query = (projected[:, :D] * scale).astype(jnp.bfloat16).reshape(quad)
    keys = projected[:, D : 2 * D].astype(jnp.bfloat16).reshape(quad)
    values = projected[:, 2 * D :].astype(jnp.bfloat16).reshape(quad)
    bias = position_bias(widen(position_table), buckets)
    valid = (jnp.arange(SLOT, dtype=jnp.int32)[None, :] < lengths[:, None])[:, None, None, :]
    logits = jnp.einsum("sqhd,skhd->shqk", query, keys, preferred_element_type=jnp.float32)
    scores = jnp.where(valid, logits + bias, masked_score)
    row_top = jnp.max(scores, -1, keepdims=True)
    shifted = jnp.exp(scores - row_top)
    row_total = jnp.sum(shifted, -1, keepdims=True)
    probs = shifted / row_total
    log_total = row_top + jnp.log(row_total)
    attended = jnp.einsum(
        "shqk,skhd->sqhd", probs.astype(jnp.bfloat16), values, preferred_element_type=jnp.float32
    )
    mixed = mix_norm(attended, scales, widen(mix_gain), widen(mix_shift)).astype(jnp.bfloat16)
    middle = (
        inputs + jnp.dot(mixed, out_weight, preferred_element_type=jnp.float32) + widen(out_bias)
    )
    second = layer_norm(middle, widen(second_gain), widen(second_shift)).astype(jnp.bfloat16)
    hidden = jnp.dot(second, up_weight, preferred_element_type=jnp.float32) + widen(up_bias)
    activated = hidden_norm(hidden, widen(hidden_gain), widen(hidden_shift)).astype(jnp.bfloat16)
    result = (
        middle
        + jnp.dot(activated, down_weight, preferred_element_type=jnp.float32)
        + widen(down_bias)
    )
    return (
        normed,
        query,
        keys,
        values,
        bias,
        valid,
        log_total,
        attended,
        mixed,
        middle,
        second,
        hidden,
        activated,
        result,
    )


def body(
    tokens,
    cotangent,
    lengths,
    buckets,
    qkv_weight,
    query_value_bias,
    out_weight,
    out_bias,
    up_weight,
    up_bias,
    down_weight,
    down_bias,
    first_gain,
    first_shift,
    mix_gain,
    mix_shift,
    second_gain,
    second_shift,
    hidden_gain,
    hidden_shift,
    head_scale,
    position_table,
):
    pieces = (
        qkv_weight,
        query_value_bias,
        out_weight,
        out_bias,
        up_weight,
        up_bias,
        down_weight,
        down_bias,
        first_gain,
        first_shift,
        mix_gain,
        mix_shift,
        second_gain,
        second_shift,
        hidden_gain,
        hidden_shift,
        position_table,
    )
    inputs = tokens.astype(jnp.float32)
    scales = widen(head_scale)
    gathered = gather_weights(pieces)
    result = forward_pass(inputs, gathered, scales, lengths, buckets)[13]
    result_tokens = result.astype(jnp.bfloat16)
    again = gather_weights(pieces)
    (
        qkv_full,
        pair_full,
        out_full,
        out_bias_full,
        up_full,
        up_bias_full,
        down_full,
        down_bias_full,
        first_gain_full,
        first_shift_full,
        mix_gain_full,
        mix_shift_full,
        second_gain_full,
        second_shift_full,
        hidden_gain_full,
        hidden_shift_full,
        table_full,
    ) = again
    (
        normed,
        query,
        keys,
        values,
        bias,
        valid,
        log_total,
        attended,
        mixed,
        middle,
        second,
        hidden,
        activated,
        unused_result,
    ) = forward_pass(inputs, again, scales, lengths, buckets)
    rows = inputs.shape[0]
    scale = HEAD_DIM ** (-0.5)
    cot_float = widen(cotangent)
    down_grad = outer_product(activated, cotangent)
    down_bias_grad = jnp.sum(cot_float, 0)
    act_grad = inner_product(cotangent, down_full)
    unused_out, pull = jax.vjp(
        hidden_norm, hidden, widen(hidden_gain_full), widen(hidden_shift_full)
    )
    hidden_grad, hidden_gain_grad, hidden_shift_grad = pull(act_grad)
    hidden_low = hidden_grad.astype(jnp.bfloat16)
    up_grad = outer_product(second, hidden_low)
    up_bias_grad = jnp.sum(widen(hidden_low), 0)
    second_in = inner_product(hidden_low, up_full)
    unused_out, pull = jax.vjp(
        layer_norm, middle, widen(second_gain_full), widen(second_shift_full)
    )
    middle_part, second_gain_grad, second_shift_grad = pull(second_in)
    middle_grad = cot_float + middle_part
    branch_low = middle_grad.astype(jnp.bfloat16)
    out_grad = outer_product(mixed, branch_low)
    out_bias_grad = jnp.sum(widen(branch_low), 0)
    mixed_in = inner_product(branch_low, out_full)
    unused_out, pull = jax.vjp(
        mix_norm, attended, scales, widen(mix_gain_full), widen(mix_shift_full)
    )
    attended_grad, scale_local, mix_gain_grad, mix_shift_grad = pull(mixed_in)
    attended_low = attended_grad.astype(jnp.bfloat16)
    logits = jnp.einsum("sqhd,skhd->shqk", query, keys, preferred_element_type=jnp.float32)
    scores = jnp.where(valid, logits + bias, masked_score)
    probs = jnp.exp(scores - log_total)
    probs_grad = jnp.einsum(
        "sqhd,skhd->shqk", attended_low, values, preferred_element_type=jnp.float32
    )
    values_grad = jnp.einsum(
        "shqk,sqhd->skhd",
        probs.astype(jnp.bfloat16),
        attended_low,
        preferred_element_type=jnp.float32,
    )
    row_dot = jnp.sum(probs * probs_grad, -1, keepdims=True)
    scores_grad = probs * (probs_grad - row_dot)
    scores_low = scores_grad.astype(jnp.bfloat16)
    query_grad = jnp.einsum("shqk,skhd->sqhd", scores_low, keys, preferred_element_type=jnp.float32)
    keys_grad = jnp.einsum("shqk,sqhd->skhd", scores_low, query, preferred_element_type=jnp.float32)
    small_pick = (buckets == 0).astype(jnp.float32)
    small_sum = jnp.einsum("s,shqk->hqk", small_pick, scores_grad)
    large_sum = jnp.einsum("s,shqk->hqk", 1.0 - small_pick, scores_grad)
    unused_out, pull = jax.vjp(bias_grids, widen(table_full))
    table_grad = pull((small_sum, large_sum))[0]
    proj_grad = jnp.concatenate(
        [
            (query_grad * scale).astype(jnp.bfloat16).reshape(rows, D),
            keys_grad.astype(jnp.bfloat16).reshape(rows, D),
            values_grad.astype(jnp.bfloat16).reshape(rows, D),
        ],
        1,
    )
    qkv_grad = outer_product(normed, proj_grad)
    column_sums = jnp.sum(widen(proj_grad), 0)
    pair_grad = jnp.concatenate([column_sums[:D], column_sums[2 * D :]])
    first_in = inner_product(proj_grad, qkv_full)
    unused_out, pull = jax.vjp(layer_norm, inputs, widen(first_gain_full), widen(first_shift_full))
    input_part, first_gain_grad, first_shift_grad = pull(first_in)
    input_grad = (middle_grad + input_part).astype(jnp.bfloat16)
    owned = scatter_grads(
        (
            qkv_grad,
            pair_grad,
            out_grad,
            out_bias_grad,
            up_grad,
            up_bias_grad,
            down_grad,
            down_bias_grad,
            first_gain_grad,
            first_shift_grad,
            mix_gain_grad,
            mix_shift_grad,
            second_gain_grad,
            second_shift_grad,
            hidden_gain_grad,
            hidden_shift_grad,
            table_grad,
        )
    )
    scale_grad = lax.psum(scale_local, ("fsdp", "dp"))
    return (
        result_tokens,
        input_grad,
        owned[0],
        owned[1],
        owned[2],
        owned[3],
        owned[4],
        owned[5],
        owned[6],
        owned[7],
        owned[8],
        owned[9],
        owned[10],
        owned[11],
        owned[12],
        owned[13],
        owned[14],
        owned[15],
        scale_grad,
        owned[16],
    )


def solution(mesh):
    in_specs = (
        P(("fsdp", "dp"), None),
        P(("fsdp", "dp"), None),
        P(("fsdp", "dp")),
        P(("fsdp", "dp")),
        P("fsdp", "dp"),
        P("fsdp"),
        P("fsdp", "dp"),
        P("fsdp"),
        P("fsdp", "dp"),
        P("fsdp"),
        P("fsdp", "dp"),
        P("fsdp"),
        P("fsdp"),
        P("fsdp"),
        P("fsdp"),
        P("fsdp"),
        P("fsdp"),
        P("fsdp"),
        P("fsdp"),
        P("fsdp"),
        P(),
        P("fsdp", None),
    )
    out_specs = (
        P(("fsdp", "dp"), None),
        P(("fsdp", "dp"), None),
        P("fsdp", "dp"),
        P("fsdp"),
        P("fsdp", "dp"),
        P("fsdp"),
        P("fsdp", "dp"),
        P("fsdp"),
        P("fsdp", "dp"),
        P("fsdp"),
        P("fsdp"),
        P("fsdp"),
        P("fsdp"),
        P("fsdp"),
        P("fsdp"),
        P("fsdp"),
        P("fsdp"),
        P("fsdp"),
        P(),
        P("fsdp", None),
    )
    return jax.shard_map(body, mesh=mesh, in_specs=in_specs, out_specs=out_specs, check_vma=False)
```

profile of v0, /device:TPU:0, one launch (start us, length us, event | category | flops | bytes accessed | tf_op | source)
XLA Modules:
  0.0 1372.2 jit_solution(17114737619744475889)
XLA Ops:
  8.9 35.7 %all_gather.85 = bf16[768,576]{1,0:T(8,128)(2,1)S(1)} all-gather(bf16[96,576]{1,0:T(8,128)(2,1)} %param.26), channel_id=1, replica_groups=mesh['fsdp'=8,'dp'=4] {'fsdp'}, dimensions={0}, use_global_device_ids=true | all-gather | bytes 995328 | tf_op jit(solution)/shard_map/all_gather | solution.py:102
  45.9 31.3 %all_gather.91 = bf16[768,192]{1,0:T(8,128)(2,1)S(1)} all-gather(bf16[96,192]{1,0:T(8,128)(2,1)S(1)} %copy-done.50), channel_id=1, replica_groups=mesh['fsdp'=8,'dp'=4] {'fsdp'}, dimensions={0}, use_global_device_ids=true | all-gather | bytes 331776 | tf_op jit(solution)/shard_map/all_gather | solution.py:103
  82.7 37.9 %all-reduce.43 = (bf16[1536]{0:T(1024)(128)(2,1)S(1)}, bf16[768]{0:T(1024)(128)(2,1)}, bf16[768]{0:T(1024)(128)(2,1)}, bf16[768]{0:T(1024)(128)(2,1)S(1)}, bf16[...) all-reduce(bf16[1536]{0:T(1024)(128)(2,1)S(1)} %dynamic-update-slic, ...), channel_id=1, replica_groups=mesh['fsdp'=8,'dp'=4] {'fsdp'}, use_global_device_ids=true, to_apply=%add.22 | all-reduce | flops 7680 | bytes 30720
  121.2 30.8 %all-gather = bf16[8,192,12]{1,2,0:T(8,128)(2,1)S(1)} all-gather(bf16[1,192,12]{1,2,0:T(8,128)(2,1)S(1)} %bitcast.182), channel_id=1, replica_groups=mesh['fsdp'=8,'dp'=4] {'fsdp'}, dimensions={0}, use_global_device_ids=true | all-gather | bytes 41472 | tf_op jit(solution)/shard_map/all_gather | solution.py:118
  178.6 12.2 tile.25
  232.2 18.4 %tile.29 = f32[12,15,15,496]{3,2,1,0:T(8,128)} reshape(f32[12,15,15,16,31]{4,3,2,1,0:T(8,128)} %tile.28) | data formatting | bytes 10713600 | tf_op jit(solution)/shard_map/tile | solution.py:24
  257.3 18.0 %reshape.447 = f32[12,15,15,15,30]{4,3,2,1,0:T(8,128)} reshape(f32[12,15,15,450]{3,2,1,0:T(8,128)} %slice.128) | data formatting | bytes 9720000 | tf_op jit(solution)/shard_map/reshape | solution.py:26
  275.3 16.3 %slice_bitcast_fusion = f32[12,15,15,15,15]{3,1,4,2,0:T(8,128)} fusion(f32[12,15,15,15,30]{4,3,2,1,0:T(8,128)} %reshape.447), kind=kLoop, calls=%fused_computation | loop fusion | bytes 4860000 | tf_op jit(solution)/shard_map/transpose | solution.py:37
  291.6 25.8 %copy.272 = f32[12,15,15,15,15]{4,3,2,1,0:T(8,128)} copy(f32[12,15,15,15,15]{3,1,4,2,0:T(8,128)} %slice_bitcast_fusion) | data formatting | bytes 4860000 | tf_op jit(solution)/shard_map/transpose | solution.py:37
  317.5 14.5 %reshape.448 = f32[12,225,225]{2,1,0:T(8,128)} reshape(f32[12,15,15,15,15]{4,3,2,1,0:T(8,128)} %copy.272) | data formatting | bytes 4860000 | tf_op jit(solution)/shard_map/reshape | solution.py:37
  345.3 25.9 %all-gather.1 = bf16[8,1,384]{2,1,0:T(2,128)(2,1)S(1)} all-gather(bf16[1,1,384]{2,1,0:T(2,128)(2,1)S(1)} %reshape.499), channel_id=1, replica_groups=mesh['fsdp'=8,'dp'=4] {'fsdp'}, dimensions={0}, use_global_device_ids=true | all-gather | bytes 6912 | tf_op jit(solution)/shard_map/all_gather | solution.py:108
  371.3 25.9 %all-gather.2 = bf16[8,1,384]{2,1,0:T(2,128)(2,1)S(1)} all-gather(bf16[1,1,384]{2,1,0:T(2,128)(2,1)S(1)} %reshape.501), channel_id=1, replica_groups=mesh['fsdp'=8,'dp'=4] {'fsdp'}, dimensions={0}, use_global_device_ids=true | all-gather | bytes 6912 | tf_op jit(solution)/shard_map/all_gather | solution.py:116
  397.2 25.9 %all-gather.3 = bf16[8,1,384]{2,1,0:T(2,128)(2,1)S(1)} all-gather(bf16[1,1,384]{2,1,0:T(2,128)(2,1)S(1)} %reshape.503), channel_id=1, replica_groups=mesh['fsdp'=8,'dp'=4] {'fsdp'}, dimensions={0}, use_global_device_ids=true | all-gather | bytes 6912 | tf_op jit(solution)/shard_map/all_gather | solution.py:117
  487.2 39.4 %fusion.75 = (f32[1024]{0:T(1024)S(1)}, f32[1024,3072]{1,0:T(8,128)}, f32[1024,3072]{1,0:T(8,128)}, f32[1024,3072]{1,0:T(8,128)}) fusion(f32[3072]{0:T(1024)S(1)} %bitcast.173, bf16[768,3072]{1,0:T(8,128)(2,1)} %all-gather.17.cloned.1.call-done, f32[1024,768]{0,1:T(8,128)} %copy-done.8, f32[768]{0:T(1024)S(1)} %convert_element_type.187, ...), kind=kOutput, calls=%fused_computation.158 | convolution fusion | flops 5043387392 | bytes 45643776 | tf_op jit(solution)/shard_map/dot_general | solution.py:236
  526.7 14.0 %multiply_reduce_fusion.2 = (f32[1024]{0:T(1024)S(1)}, f32[1024]{0:T(1024)S(1)}, f32[3072]{0:T(1024)}, f32[1024,3072]{1,0:T(8,128)}) fusion(f32[1024,3072]{1,0:T(8,128)} %get-tuple-element.195, f32[3072]{0:T(1024)S(1)} %bitcast.170, f32[1024]{0:T(1024)S(1)} %broadcast_multiply_fusion, bf16[1024,768]{1,0:T(8,128)(2,1)S(1)} %copy-done.31, ...), kind=kOutput, calls=%fused_computation.10 | convolution fusion | flops 4853853184 | bytes 31494144 | tf_op jit(solution)/shard_map/dot_general | solution.py:65
  549.7 19.6 %convert_reduce_fusion = (f32[3072]{0:T(1024)}, bf16[1024,3072]{1,0:T(8,128)(2,1)S(1)}, bf16[1024,3072]{1,0:T(8,128)(2,1)}) fusion(f32[1024,3072]{1,0:T(8,128)} %get-tuple-element.196, f32[1024]{0:T(1024)S(1)} %negate_multiply_fusion.4, f32[1024]{0:T(1024)S(1)} %get-tuple-element.208, f32[1024,3072]{1,0:T(8,128)S(1)} %bitcast.152, ...), kind=kLoop, calls=%fused_computation.5 | loop fusion | flops 88077312 | bytes 62980096 | tf_op jit(solution)/shard_map/reduce_sum | solution.py:357
  569.2 12.0 fusion.86
  725.3 13.7 reshape.469
  793.7 13.6 reshape.461
  812.9 15.3 %reshape.454 = f32[12,15,15,15,15]{4,3,2,1,0:T(8,128)} reshape(f32[12,225,225]{2,1,0:T(8,128)} %slice_select_fusion) | data formatting | bytes 4860000 | tf_op jit(solution)/shard_map/transpose(jvp())/reshape | solution.py:37
  828.2 28.1 %copy.297 = f32[12,15,15,15,15]{3,1,4,2,0:T(8,128)} copy(f32[12,15,15,15,15]{4,3,2,1,0:T(8,128)} %reshape.454) | data formatting | bytes 4860000 | tf_op jit(solution)/shard_map/transpose(jvp())/reshape | solution.py:37
  856.2 16.5 %pad.77 = f32[12,15,15,15,30]{4,3,2,1,0:T(8,128)} pad(f32[12,15,15,15,15]{4,3,2,1,0:T(8,128)} %bitcast.150, f32[]{:T(128)} %constant.41.clone.1), padding=0_0x0_0x0_0x0_0x0_15 | pad | bytes 7290004 | tf_op jit(solution)/shard_map/transpose(jvp())/pad | solution.py:26
  872.8 17.9 %reshape.455 = f32[12,15,15,450]{3,2,1,0:T(8,128)} reshape(f32[12,15,15,15,30]{4,3,2,1,0:T(8,128)} %pad.77) | data formatting | bytes 9720000 | tf_op jit(solution)/shard_map/transpose(jvp())/reshape | solution.py:26
  897.4 18.8 %reshape.456 = f32[12,15,15,16,31]{4,3,2,1,0:T(8,128)} reshape(f32[12,15,15,496]{3,2,1,0:T(8,128)} %pad.78) | data formatting | bytes 10713600 | tf_op jit(solution)/shard_map/transpose(jvp())/reshape | solution.py:24
  916.2 11.0 reduce_sum.378
  965.2 38.7 %psum.110 = f32[12]{0:T(128)} all-reduce(f32[12]{0:T(128)S(1)} %fusion.26), channel_id=1, replica_groups=mesh['fsdp'=8,'dp'=4] {'fsdp','dp'}, use_global_device_ids=true, to_apply=%region_64.65 | all-reduce | flops 12 | bytes 96 | tf_op jit(solution)/shard_map/psum | solution.py:431
  1028.5 56.7 %reduce-scatter.32.cloned.1.call-done = f32[192,12]{1,0:T(8,128)} async-done(((f32[1536,12]{1,0:T(8,128)}), f32[192,12]{1,0:T(8,128)}) %reduce-scatter.32.cloned.1.call-update) | async-done | bytes 9232
  1086.2 10.9 all-reduce.42
  1097.1 53.8 %reduce-scatter.30.cloned.1.call-done = f32[96,192]{1,0:T(8,128)} async-done(((f32[768,192]{1,0:T(8,128)}), f32[96,192]{1,0:T(8,128)}) %reduce-scatter.30.cloned.1.call-update) | async-done | bytes 73744
  1150.8 69.7 %reduce-scatter.28.cloned.1.call-done = f32[96,576]{1,0:T(8,128)} async-done(((f32[768,576]{1,0:T(8,128)}), f32[96,576]{1,0:T(8,128)}) %reduce-scatter.28.cloned.1.call-update) | async-done | bytes 221200
  1220.6 72.4 %reduce-scatter.22.cloned.1.call-done = f32[96,768]{1,0:T(8,128)} async-done(((f32[768,768]{1,0:T(8,128)}), f32[96,768]{1,0:T(8,128)}) %reduce-scatter.22.cloned.1.call-update) | async-done | bytes 294928 | tf_op jit(solution)/shard_map/reduce_scatter | solution.py:148
  1293.0 72.5 %reduce-scatter.26.cloned.1.call-done = f32[384,192]{0,1:T(8,128)} async-done(((f32[3072,192]{0,1:T(8,128)}), f32[384,192]{0,1:T(8,128)}) %reduce-scatter.26.cloned.1.call-update) | async-done | bytes 294928 | tf_op jit(solution)/shard_map/reduce_scatter | solution.py:149
  (454 shorter events, 440.0 us)
Async XLA Ops:
  7.2 70.9 %all-gather.15.cloned.1.call-start = ((), (), s32[]{:S(2)}) async-start(), calls=%async_computation.11 | async-start | bytes 1327104 | tf_op jit(solution)/shard_map/all_gather | solution.py:104
  7.9 418.3 %all-gather.19.cloned.1.call-start = ((), (), s32[]{:S(2)}) async-start(), calls=%async_computation.13 | async-start | bytes 1327104 | tf_op jit(solution)/shard_map/all_gather | solution.py:105
  8.7 72.3 %copy-start.77 = (bf16[96]{0:T(256)(128)(2,1)S(1)}, bf16[96]{0:T(256)(128)(2,1)}, u32[]{:S(2)}) copy-start(bf16[96]{0:T(256)(128)(2,1)} %param.29) | copy-start | bytes 580
  8.7 72.5 %copy-start.78 = (bf16[96]{0:T(256)(128)(2,1)S(1)}, bf16[96]{0:T(256)(128)(2,1)}, u32[]{:S(2)}) copy-start(bf16[96]{0:T(256)(128)(2,1)} %param.37) | copy-start | bytes 580
  8.7 72.8 %copy-start.79 = (bf16[96]{0:T(256)(128)(2,1)S(1)}, bf16[96]{0:T(256)(128)(2,1)}, u32[]{:S(2)}) copy-start(bf16[96]{0:T(256)(128)(2,1)} %param.36) | copy-start | bytes 580
  8.8 73.0 %copy-start.80 = (bf16[96]{0:T(256)(128)(2,1)S(1)}, bf16[96]{0:T(256)(128)(2,1)}, u32[]{:S(2)}) copy-start(bf16[96]{0:T(256)(128)(2,1)} %param.39) | copy-start | bytes 580
  8.8 73.2 %copy-start.81 = (bf16[96]{0:T(256)(128)(2,1)S(1)}, bf16[96]{0:T(256)(128)(2,1)}, u32[]{:S(2)}) copy-start(bf16[96]{0:T(256)(128)(2,1)} %param.38) | copy-start | bytes 580
  8.8 73.4 %copy-start.82 = (bf16[96]{0:T(256)(128)(2,1)S(1)}, bf16[96]{0:T(256)(128)(2,1)}, u32[]{:S(2)}) copy-start(bf16[96]{0:T(256)(128)(2,1)} %param.33) | copy-start | bytes 580
  8.8 73.7 %copy-start.83 = (bf16[192]{0:T(256)(128)(2,1)S(1)}, bf16[192]{0:T(256)(128)(2,1)}, u32[]{:S(2)}) copy-start(bf16[192]{0:T(256)(128)(2,1)} %param.27) | copy-start | bytes 1156
  8.8 112.4 %copy-start.84 = (bf16[12]{0:T(256)(128)(2,1)S(1)}, bf16[12]{0:T(256)(128)(2,1)}, u32[]{:S(2)}) copy-start(bf16[12]{0:T(256)(128)(2,1)} %param.42) | copy-start | bytes 76
  8.8 112.4 %copy-start.60 = (bf16[192,12]{0,1:T(8,128)(2,1)S(1)}, bf16[192,12]{0,1:T(8,128)(2,1)}, u32[]{:S(2)}) copy-start(bf16[192,12]{0,1:T(8,128)(2,1)} %param.43) | copy-start | bytes 13828
  8.8 417.6 %all-gather.11.cloned.1.call-start = ((), (), s32[]{:S(2)}) async-start(), calls=%async_computation.9 | async-start | bytes 4423680 | tf_op jit(solution)/shard_map/all_gather | solution.py:121
  45.8 435.4 %all-gather.13.cloned.1.call-start = ((), (), s32[]{:S(2)}) async-start(), calls=%async_computation.10 | async-start | bytes 1474560 | tf_op jit(solution)/shard_map/all_gather | solution.py:122
  78.0 409.2 %all-gather.17.cloned.1.call-start = ((), (), s32[]{:S(2)}) async-start(), calls=%async_computation.12 | async-start | bytes 5898240 | tf_op jit(solution)/shard_map/all_gather | solution.py:123
  78.6 448.0 %all-gather.21.cloned.1.call-start = ((), (), s32[]{:S(2)}) async-start(), calls=%async_computation.14 | async-start | bytes 5898240 | tf_op jit(solution)/shard_map/all_gather | solution.py:124
  121.2 345.5 %copy-start.61 = (f32[12]{0:T(128)}, f32[12]{0:T(128)S(1)}, u32[]{:S(2)}) copy-start(f32[12]{0:T(128)S(1)} %convert_element_type.181) | copy-start | bytes 148
  343.3 80.5 %copy-start.30 = (bf16[1024,768]{1,0:T(8,128)(2,1)S(1)}, bf16[1024,768]{1,0:T(8,128)(2,1)}, u32[]{:S(2)}) copy-start(bf16[1024,768]{1,0:T(8,128)(2,1)} %param.23) | copy-start | bytes 4718596
  345.1 136.1 %copy-start.4 = (bf16[1024,768]{0,1:T(8,128)(2,1)}, bf16[1024,768]{0,1:T(8,128)(2,1)S(1)}, u32[]{:S(2)}) copy-start(bf16[1024,768]{0,1:T(8,128)(2,1)S(1)} %copy.258) | copy-start | bytes 4718596
  345.2 80.5 %copy-start.86 = (s32[4]{0:T(128)S(1)}, s32[4]{0:T(128)}, u32[]{:S(2)}) copy-start(s32[4]{0:T(128)} %param.25) | copy-start | bytes 52
  345.2 80.5 %copy-start.85 = (s32[4]{0:T(128)S(1)}, s32[4]{0:T(128)}, u32[]{:S(2)}) copy-start(s32[4]{0:T(128)} %param.24) | copy-start | bytes 52
  345.2 81.2 %copy-start.63 = (f32[768]{0:T(1024)}, f32[768]{0:T(1024)S(1)}, u32[]{:S(2)}) copy-start(f32[768]{0:T(1024)S(1)} %convert_element_type.175) | copy-start | bytes 9220
  345.2 81.2 %copy-start.46 = (f32[768]{0:T(1024)}, f32[768]{0:T(1024)S(1)}, u32[]{:S(2)}) copy-start(f32[768]{0:T(1024)S(1)} %convert_element_type.174) | copy-start | bytes 9220
  426.3 523.3 %reduce-scatter.18.cloned.1.call-start = ((), (), s32[]{:S(2)}) async-start(), calls=%async_computation.16 | async-start | bytes 1474560 | tf_op jit(solution)/shard_map/reduce_scatter | solution.py:135
  627.8 324.0 %reduce-scatter.16.cloned.1.call-start = ((), (), s32[]{:S(2)}) async-start(), calls=%async_computation.15 | async-start | bytes 4423680 | tf_op jit(solution)/shard_map/reduce_scatter | solution.py:132
  652.9 301.5 %reduce-scatter.20.cloned.1.call-start = ((), (), s32[]{:S(2)}) async-start(), calls=%async_computation.17 | async-start | bytes 5898240 | tf_op jit(solution)/shard_map/reduce_scatter | solution.py:138
  664.5 292.9 %reduce-scatter.24.cloned.1.call-start = ((), (), s32[]{:S(2)}) async-start(), calls=%async_computation.19 | async-start | bytes 5898240 | tf_op jit(solution)/shard_map/reduce_scatter | solution.py:141
  675.6 343.9 %all-reduce.46.cloned.1.call-start = ((), (), s32[]{:S(2)}) async-start(), calls=%async_computation.24 | async-start | bytes 155648
  948.3 137.0 %reduce-scatter.32.cloned.1.call-start = ((), (), s32[]{:S(2)}) async-start(), calls=%async_computation.23 | async-start | bytes 884736
  949.6 201.3 %reduce-scatter.30.cloned.1.call-start = ((), (), s32[]{:S(2)}) async-start(), calls=%async_computation.22 | async-start | bytes 884736
  951.7 268.8 %reduce-scatter.28.cloned.1.call-start = ((), (), s32[]{:S(2)}) async-start(), calls=%async_computation.21 | async-start | bytes 2211840
  954.4 338.6 %reduce-scatter.22.cloned.1.call-start = ((), (), s32[]{:S(2)}) async-start(), calls=%async_computation.18 | async-start | bytes 2654208 | tf_op jit(solution)/shard_map/reduce_scatter | solution.py:148
  957.4 408.1 %reduce-scatter.26.cloned.1.call-start = ((), (), s32[]{:S(2)}) async-start(), calls=%async_computation.20 | async-start | bytes 2654208 | tf_op jit(solution)/shard_map/reduce_scatter | solution.py:149
  (78 other events, 709.7 us)
Sparse Core Ops, SparseCore 0:
  10.2 48.7 all-gather.14
  61.1 41.0 all-gather.18
  104.3 29.0 all-gather.10
  135.4 17.4 all-gather.12
  154.3 37.4 all-gather.16
  426.4 34.7 all-gather.20
  627.9 23.0 reduce-scatter.17
  653.7 40.4 reduce-scatter.15
  696.8 47.8 reduce-scatter.19
  747.2 47.8 reduce-scatter.23
  948.4 71.0 all-reduce.45
  1022.6 62.5 reduce-scatter.31
  1089.4 61.3 reduce-scatter.29
  1154.7 65.7 reduce-scatter.27
  1224.9 68.0 reduce-scatter.21
  1297.3 68.1 reduce-scatter.25
where the time goes:
time: 1380 us; the launch traced here: 1370 us
  local copies, waits for them, and re-layouts  482 us (35%)
  waiting for transfers between devices  330 us (24%)
  blocking collectives  263 us (19%)
  matrix products  171 us (12%)
  other arithmetic  106 us (8%)
  between operations  19.1 us (1%)
    unnamed x20, waiting for transfers between devices  185 us
    reshape x12, local copies, waits for them, and re-layouts, toeplitz(): return band.reshape(line.shape[:-1] + (count, width - 1))[..., :count]  76.9 us
    reduce_scatter x1, waiting for transfers between devices, scatter_grads(): lax.psum_scatter(cols[3], 'fsdp', scatter_dimension=0, tiled=True)  72.5 us
    reduce_scatter x1, waiting for transfers between devices, scatter_grads(): lax.psum_scatter(cols[2], 'fsdp', scatter_dimension=0, tiled=True)  72.4 us
    reshape x5, local copies, waits for them, and re-layouts, grid_bias(): jnp.transpose(rowwise, (0, 3, 1, 4, 2)).reshape(-1, patches, patches)  61.8 us
    another operation x10, local copies, waits for them, and re-layouts, toeplitz(): tiled = jnp.tile(line, (1,) * (line.ndim - 1) + (count + 1,))  55.1 us
    reshape x6, local copies, waits for them, and re-layouts, toeplitz(): tiled = jnp.tile(line, (1,) * (line.ndim - 1) + (count + 1,))  53.7 us
    unnamed x239, local copies, waits for them, and re-layouts  47 us
  transfers between devices with their start and end apart: 16, of which 6 were waited for; matrix products, arithmetic and copies ran while one was open for 47% of the time, Pallas kernels for 0%

commit v1 on v0

v1 whole, which is shorter than its diff:
```python
import functools

import jax
import jax.numpy as jnp
from jax import lax
from jax.experimental import pallas as pl
from jax.experimental.pallas import tpu as pltpu
from jax.sharding import PartitionSpec as P

D = 768
HEADS = 12
PAIRS = 6
HEAD_DIM = 64
FF = 3072
SLOT = 256
TABLE = 1536

EPS = 1e-05
MASKED = -1000000000.0
F32 = jnp.float32
BF16 = jnp.bfloat16
VMEM_LIMIT = 60 * 2**20


def params(**more):
    return pltpu.CompilerParams(vmem_limit_bytes=VMEM_LIMIT, **more)


def nn(left, right):
    return lax.dot_general(left, right, (((1,), (0,)), ((), ())), preferred_element_type=F32)


def nt(left, right):
    return lax.dot_general(left, right, (((1,), (1,)), ((), ())), preferred_element_type=F32)


def standardize(values):
    center = values - jnp.mean(values, -1, keepdims=True)
    inverse = lax.rsqrt(jnp.mean(center * center, -1, keepdims=True) + EPS)
    return center * inverse, inverse


def norm_back(grad, unit, inverse):
    return inverse * (
        grad
        - jnp.mean(grad, -1, keepdims=True)
        - unit * jnp.mean(grad * unit, -1, keepdims=True)
    )


def column_sum(values):
    return jnp.sum(values, 0, keepdims=True)


def split_low(values):
    high = values.astype(BF16)
    return high, (values - high.astype(F32)).astype(BF16)


def compaction(side, lanes):
    plane = lax.broadcasted_iota(jnp.int32, (1024, lanes), 0)
    lane = lax.broadcasted_iota(jnp.int32, (1024, lanes), 1)
    across = plane & 31
    return ((lane == side * (plane >> 5) + across) & (across < side)).astype(F32).astype(BF16)


def inside_grid(patches):
    row = lax.broadcasted_iota(jnp.int32, (SLOT, SLOT), 0)
    col = lax.broadcasted_iota(jnp.int32, (SLOT, SLOT), 1)
    return (row < patches) & (col < patches)


def store_tiles(ref, values):
    for k in range(ref.shape[0]):
        ref[k] = values[:, 128 * k : 128 * k + 128]


def load_tiles(ref):
    return jnp.concatenate([ref[k] for k in range(ref.shape[0])], 1)


def load_strided(ref, first, count):
    return jnp.concatenate(
        [ref[k, pl.ds(first, count, 16), :] for k in range(ref.shape[0])], 1
    )


def store_strided(ref, first, values):
    for k in range(ref.shape[0]):
        ref[k, pl.ds(first, values.shape[0], 16), :] = values[:, 128 * k : 128 * k + 128]


def bias_kernel(table_ref, out_ref, wall_small, wall_large, visual):
    plane = table_ref[:, 512:]
    shifted = [pltpu.roll(plane, (ic - 15) % 1024, 1) for ic in range(16)]
    stack = jnp.concatenate(shifted, 0).astype(BF16)
    store_tiles(wall_large, nn(stack, compaction(15, 512)))
    store_tiles(wall_small, nn(stack[:128], compaction(8, 256)))
    visual[...] = jnp.zeros_like(visual)

    def one_head(h, carry):
        line = jnp.broadcast_to(table_ref[pl.ds(h, 1), :512], (SLOT, 512))
        textual = pltpu.roll(line, 257, 1, stride=1, stride_axis=0)[:, :SLOT]
        large = load_strided(wall_large, h, 16)
        for ir in range(15):
            visual[pl.ds(ir * 15, 16), :] = pltpu.roll(large, 512 - (15 - ir) * 15, 1)[:, :SLOT]
        out_ref[1, h] = jnp.where(inside_grid(225), visual[...], textual).astype(BF16)
        small = load_strided(wall_small, h, 8)
        rows = [pltpu.roll(small, 256 - (15 - ir) * 8, 1) for ir in range(8)]
        grid = jnp.concatenate(rows + [jnp.zeros((192, SLOT), F32)], 0)
        out_ref[0, h] = jnp.where(inside_grid(64), grid, textual).astype(BF16)
        return carry

    lax.fori_loop(0, HEADS, one_head, 0)


def build_bias(table):
    return pl.pallas_call(
        bias_kernel,
        out_shape=jax.ShapeDtypeStruct((2, HEADS, SLOT, SLOT), BF16),
        scratch_shapes=[
            pltpu.VMEM((2, 128, 128), F32),
            pltpu.VMEM((4, 256, 128), F32),
            pltpu.VMEM((SLOT, SLOT), F32),
        ],
        compiler_params=params(),
        name="build_bias",
    )(table)


def table_grad_kernel(grid_ref, out_ref, wall_small, wall_large):
    wall_small[...] = jnp.zeros_like(wall_small)
    wall_large[...] = jnp.zeros_like(wall_large)
    row = lax.broadcasted_iota(jnp.int32, (SLOT, SLOT), 0)
    col = lax.broadcasted_iota(jnp.int32, (SLOT, SLOT), 1)
    flip = (row + col == SLOT - 1).astype(F32).astype(BF16)
    lane = lax.broadcasted_iota(jnp.int32, (16, SLOT), 1)

    out_ref[...] = jnp.zeros_like(out_ref)

    def one_head(h, carry):
        textual = jnp.where(inside_grid(64), 0.0, grid_ref[0, h]) + jnp.where(
            inside_grid(225), 0.0, grid_ref[1, h]
        )
        high, low = split_low(textual)
        flipped = nn(flip, high) + nn(flip, low)
        wide = jnp.concatenate([flipped, jnp.zeros((SLOT, SLOT), F32)], 1)
        out_ref[pl.ds(h, 1), :512] = column_sum(
            pltpu.roll(wide, 0, 1, stride=1, stride_axis=0)
        )
        total = jnp.zeros((16, 512), F32)
        for ir in range(15):
            part = jnp.where(lane < 225, grid_ref[1, h, pl.ds(ir * 15, 16), :], 0.0)
            part = jnp.concatenate([part, jnp.zeros((16, SLOT), F32)], 1)
            total = total + pltpu.roll(part, (15 - ir) * 15, 1)
        store_strided(wall_large, h, total)
        total = jnp.zeros((8, SLOT), F32)
        for ir in range(8):
            part = jnp.where(lane[:8] < 64, grid_ref[0, h, pl.ds(ir * 8, 8), :], 0.0)
            total = total + pltpu.roll(part, (15 - ir) * 8, 1)
        store_strided(wall_small, h, total)
        return carry

    lax.fori_loop(0, HEADS, one_head, 0)
    high, low = split_low(load_tiles(wall_large))
    spread = compaction(15, 512)
    large = nt(high, spread) + nt(low, spread)
    high, low = split_low(load_tiles(wall_small))
    spread = compaction(8, 256)
    small = nt(high, spread) + nt(low, spread)
    plane = jnp.zeros((16, 1024), F32)
    for ic in range(15):
        part = large[ic * 16 : ic * 16 + 16]
        if ic < 8:
            part = part + small[ic * 16 : ic * 16 + 16]
        plane = plane + pltpu.roll(part, 15 - ic, 1)
    out_ref[:, 512:] = plane


def table_grad(grids):
    return pl.pallas_call(
        table_grad_kernel,
        out_shape=jax.ShapeDtypeStruct((16, TABLE), F32),
        scratch_shapes=[pltpu.VMEM((2, 128, 128), F32), pltpu.VMEM((4, 256, 128), F32)],
        compiler_params=params(),
        name="table_grad",
    )(grids)


def attention_kernel(
    lengths, buckets, x_ref, vec_ref, weight_ref, qkv_bias_ref, bias_ref,
    normed_ref, qkv_ref, probs_ref, attended_ref,
):
    count = x_ref.shape[0] // SLOT

    def one_block(b, carry):
        rows = pl.ds(pl.multiple_of(b * SLOT, SLOT), SLOT)
        unit, inverse = standardize(x_ref[rows, :].astype(F32))
        normed_ref[rows, :] = (unit * vec_ref[0:1, :] + vec_ref[1:2, :]).astype(BF16)
        return carry

    lax.fori_loop(0, count, one_block, 0)

    def one_panel(n, carry):
        cols = pl.ds(pl.multiple_of(n * 256, 256), 256)
        out = nn(normed_ref[...], weight_ref[:, cols]) + qkv_bias_ref[:, cols]
        out = (out * jnp.where(n < 3, HEAD_DIM ** (-0.5), 1.0)).astype(BF16)
        qkv_ref[2 * n] = out[:, :128]
        qkv_ref[2 * n + 1] = out[:, 128:]
        return carry

    lax.fori_loop(0, 9, one_panel, 0)
    lane = lax.broadcasted_iota(jnp.int32, (SLOT, 128), 1)
    key_slot = lax.broadcasted_iota(jnp.int32, (SLOT, SLOT), 1)

    def one_unit(step, carry):
        pair = step // count
        s = step % count
        rows = pl.ds(pl.multiple_of(s * SLOT, SLOT), SLOT)
        query = qkv_ref[pair, rows, :]
        keys = qkv_ref[PAIRS + pair, rows, :]
        values = qkv_ref[2 * PAIRS + pair, rows, :]
        live = key_slot < lengths[s]
        total = jnp.zeros((SLOT, 128), F32)
        for half in range(2):
            mine = (lane >= 64 * half) & (lane < 64 * half + 64)
            logits = nt(jnp.where(mine, query, 0), keys)
            bias = bias_ref[buckets[s], 2 * pair + half].astype(F32)
            scores = jnp.where(live, logits + bias, MASKED)
            shifted = jnp.exp(scores - jnp.max(scores, -1, keepdims=True))
            probs = (shifted / jnp.sum(shifted, -1, keepdims=True)).astype(BF16)
            probs_ref[2 * pair + half, s] = probs
            total = total + nn(probs, jnp.where(mine, values, 0))
        attended_ref[rows, pl.ds(pl.multiple_of(pair * 128, 128), 128)] = total
        return carry

    lax.fori_loop(0, PAIRS * count, one_unit, 0)


def attention(lengths, buckets, tokens, vecs, weight, qkv_bias, bias):
    rows = tokens.shape[0]
    count = rows // SLOT
    smem = pl.BlockSpec(memory_space=pltpu.SMEM)
    vmem = pl.BlockSpec(memory_space=pltpu.VMEM)
    return pl.pallas_call(
        attention_kernel,
        in_specs=[smem, smem] + [vmem] * 5,
        out_shape=[
            jax.ShapeDtypeStruct((rows, D), BF16),
            jax.ShapeDtypeStruct((3 * PAIRS, rows, 128), BF16),
            jax.ShapeDtypeStruct((HEADS, count, SLOT, SLOT), BF16),
            jax.ShapeDtypeStruct((rows, D), F32),
        ],
        compiler_params=params(),
        name="attention_forward",
    )(lengths, buckets, tokens, vecs, weight, qkv_bias, bias)


PANEL = 512


def feed_kernel(
    x_ref, attended_ref, cot_ref, out_w, up_w, down_w, vec_ref, wide_ref, scale_ref,
    result_ref, mixed_ref, second_ref, act_ref, low_ref, branch_ref, middle_grad_ref,
    attended_low_ref, sums_ref, wide_sums_ref,
    gelu_ref, slope_ref, grad_ref,
):
    @pl.when(pl.program_id(0) == 0)
    def _():
        sums_ref[...] = jnp.zeros_like(sums_ref)
        wide_sums_ref[...] = jnp.zeros_like(wide_sums_ref)

    def add(row, values):
        sums_ref[row : row + 1, :] += column_sum(values)

    rows = x_ref.shape[0]
    attended = attended_ref[...]
    mix_unit, mix_inverse = standardize(attended * scale_ref[...])
    mixed = (mix_unit * vec_ref[2:3, :] + vec_ref[3:4, :]).astype(BF16)
    mixed_ref[...] = mixed
    middle = x_ref[...].astype(F32) + nn(mixed, out_w[...]) + vec_ref[6:7, :]
    second_unit, second_inverse = standardize(middle)
    second = (second_unit * vec_ref[4:5, :] + vec_ref[5:6, :]).astype(BF16)
    second_ref[...] = second
    cot = cot_ref[...]

    panels = [slice(n, n + PANEL) for n in range(0, FF, PANEL)]
    total = jnp.zeros((rows, 1), F32)
    for cols in panels:
        hidden = nn(second, up_w[:, cols]) + wide_ref[0:1, cols]
        cdf = 0.5 + 0.5 * lax.erf(hidden * 0.7071067811865476)
        gelu = hidden * cdf
        gelu_ref[:, cols] = gelu
        slope_ref[:, cols] = cdf + hidden * (jnp.exp(-0.5 * hidden * hidden) * 0.3989422804014327)
        total = total + jnp.sum(gelu, -1, keepdims=True)
    mean = total * (1.0 / FF)
    total = jnp.zeros((rows, 1), F32)
    for cols in panels:
        center = gelu_ref[:, cols] - mean
        total = total + jnp.sum(center * center, -1, keepdims=True)
    inverse = lax.rsqrt(total * (1.0 / FF) + EPS)
    result = middle + vec_ref[7:8, :]
    first = jnp.zeros((rows, 1), F32)
    second_moment = jnp.zeros((rows, 1), F32)
    for cols in panels:
        unit = (gelu_ref[:, cols] - mean) * inverse
        gelu_ref[:, cols] = unit
        act = (unit * wide_ref[1:2, cols] + wide_ref[2:3, cols]).astype(BF16)
        act_ref[:, cols] = act
        result = result + nt(act, down_w[:, cols])
        act_grad = nn(cot, down_w[:, cols])
        wide_sums_ref[1:2, cols] += column_sum(act_grad * unit)
        wide_sums_ref[2:3, cols] += column_sum(act_grad)
        grad = act_grad * wide_ref[1:2, cols]
        grad_ref[:, cols] = grad
        first = first + jnp.sum(grad, -1, keepdims=True)
        second_moment = second_moment + jnp.sum(grad * unit, -1, keepdims=True)
    result_ref[...] = result.astype(BF16)
    first = first * (1.0 / FF)
    second_moment = second_moment * (1.0 / FF)
    second_in = jnp.zeros((rows, D), F32)
    for cols in panels:
        grad = inverse * (grad_ref[:, cols] - first - gelu_ref[:, cols] * second_moment)
        low = (grad * slope_ref[:, cols]).astype(BF16)
        low_ref[:, cols] = low
        wide_sums_ref[0:1, cols] += column_sum(low.astype(F32))
        second_in = second_in + nt(low, up_w[:, cols])
    add(4, second_in * second_unit)
    add(5, second_in)
    cot_wide = cot.astype(F32)
    add(7, cot_wide)
    middle_grad = cot_wide + norm_back(second_in * vec_ref[4:5, :], second_unit, second_inverse)
    middle_grad_ref[...] = middle_grad
    branch = middle_grad.astype(BF16)
    branch_ref[...] = branch
    add(6, branch.astype(F32))
    mixed_in = nt(branch, out_w[...])
    add(2, mixed_in * mix_unit)
    add(3, mixed_in)
    grad = norm_back(mixed_in * vec_ref[2:3, :], mix_unit, mix_inverse)
    add(8, grad * attended)
    attended_low_ref[...] = (grad * scale_ref[...]).astype(BF16)


def feed_forward(tokens, attended, cotangent, out_w, up_w, down_w, vecs, wide, scales):
    rows = tokens.shape[0]
    tile = 256
    block = pl.BlockSpec((tile, D), lambda i: (i, 0))
    wide_block = pl.BlockSpec((tile, FF), lambda i: (i, 0))

    def whole(shape):
        return pl.BlockSpec(shape, lambda i: (0, 0), pipeline_mode=pl.Buffered(1))

    def held(shape):
        return pl.BlockSpec(shape, lambda i: (0, 0))

    return pl.pallas_call(
        feed_kernel,
        grid=(rows // tile,),
        in_specs=[block] * 3
        + [whole((D, D)), whole((D, FF)), whole((D, FF)), whole((8, D)), whole((8, FF)), whole((1, D))],
        out_specs=[block, block, block, wide_block, wide_block, block, block, block]
        + [held((16, D)), held((8, FF))],
        out_shape=[
            jax.ShapeDtypeStruct((rows, D), BF16),
            jax.ShapeDtypeStruct((rows, D), BF16),
            jax.ShapeDtypeStruct((rows, D), BF16),
            jax.ShapeDtypeStruct((rows, FF), BF16),
            jax.ShapeDtypeStruct((rows, FF), BF16),
            jax.ShapeDtypeStruct((rows, D), BF16),
            jax.ShapeDtypeStruct((rows, D), F32),
            jax.ShapeDtypeStruct((rows, D), BF16),
            jax.ShapeDtypeStruct((16, D), F32),
            jax.ShapeDtypeStruct((8, FF), F32),
        ],
        scratch_shapes=[pltpu.VMEM((tile, FF), F32)] * 3,
        compiler_params=params(dimension_semantics=("arbitrary",)),
        name="feed_forward",
    )(tokens, attended, cotangent, out_w, up_w, down_w, vecs, wide, scales)


def outer_kernel(left_ref, right_ref, out_ref, turned):
    @pl.when(pl.program_id(0) == 0)
    def _():
        turned[...] = left_ref[...].T

    out_ref[...] = nn(turned[...], right_ref[...]).astype(BF16)


def outer_product(left, right, panel):
    rows, width = left.shape
    cols = right.shape[1]
    return pl.pallas_call(
        outer_kernel,
        grid=(cols // panel,),
        in_specs=[
            pl.BlockSpec((rows, width), lambda i: (0, 0), pipeline_mode=pl.Buffered(1)),
            pl.BlockSpec((rows, panel), lambda i: (0, i)),
        ],
        out_specs=pl.BlockSpec((width, panel), lambda i: (0, i)),
        out_shape=jax.ShapeDtypeStruct((width, cols), BF16),
        scratch_shapes=[pltpu.VMEM((width, rows), BF16)],
        compiler_params=params(dimension_semantics=("arbitrary",)),
        name="weight_grad",
    )(left, right)


def attention_back_kernel(
    buckets, probs_ref, query_ref, keys_ref, values_ref, low_ref, normed_ref, x_ref, middle_ref,
    weight_q, weight_k, weight_v, vec_ref,
    input_grad_ref, grid_ref, weight_grad_ref, pair_ref, sums_ref,
    turned, first_in, proj_ref,
):
    count = x_ref.shape[0] // SLOT
    step = pl.program_id(0)

    @pl.when(step == 0)
    def _():
        turned[...] = normed_ref[...].T
        first_in[...] = jnp.zeros_like(first_in)

    grid_ref[...] = jnp.zeros_like(grid_ref)
    lane = lax.broadcasted_iota(jnp.int32, (SLOT, 128), 1)

    def one_sequence(s, carry):
        rows = pl.ds(pl.multiple_of(s * SLOT, SLOT), SLOT)
        query = query_ref[0, rows, :]
        keys = keys_ref[0, rows, :]
        values = values_ref[0, rows, :]
        grad = low_ref[rows, :]
        query_turned = query.T
        grad_turned = grad.T
        small = jnp.where(buckets[s] == 0, 1.0, 0.0)
        query_grad = jnp.zeros((SLOT, 128), F32)
        keys_parts = []
        values_parts = []
        for half in range(2):
            mine = (lane >= 64 * half) & (lane < 64 * half + 64)
            part = slice(64 * half, 64 * half + 64)
            low = probs_ref[half, s]
            probs = low.astype(F32)
            probs_grad = nt(jnp.where(mine, grad, 0), values)
            values_parts.append(nn(grad_turned[part], low))
            row_dot = jnp.sum(probs * probs_grad, -1, keepdims=True)
            scores_grad = probs * (probs_grad - row_dot)
            grid_ref[0, half] += scores_grad * small
            grid_ref[1, half] += scores_grad * (1.0 - small)
            scores_low = scores_grad.astype(BF16)
            query_grad = query_grad + nn(scores_low, jnp.where(mine, keys, 0))
            keys_parts.append(nn(query_turned[part], scores_low))
        proj_ref[rows, 0:128] = (query_grad * HEAD_DIM ** (-0.5)).astype(BF16)
        proj_ref[rows, 128:256] = jnp.concatenate(keys_parts, 0).T.astype(BF16)
        proj_ref[rows, 256:384] = jnp.concatenate(values_parts, 0).T.astype(BF16)
        return carry

    lax.fori_loop(0, count, one_sequence, 0)
    proj = proj_ref[...]
    weight_grad_ref[0] = nn(turned[...], proj).astype(BF16)
    pair_ref[0] = jnp.broadcast_to(column_sum(proj.astype(F32)), (8, 384))
    weights = jnp.concatenate([weight_q[...], weight_k[...], weight_v[...]], 1)
    first_in[...] += nt(proj, weights)

    @pl.when(step == PAIRS - 1)
    def _():
        sums_ref[...] = jnp.zeros_like(sums_ref)

        def one_block(b, carry):
            rows = pl.ds(pl.multiple_of(b * SLOT, SLOT), SLOT)
            unit, inverse = standardize(x_ref[rows, :].astype(F32))
            grad = first_in[rows, :]
            sums_ref[0:1, :] += column_sum(grad * unit)
            sums_ref[1:2, :] += column_sum(grad)
            back = norm_back(grad * vec_ref[0:1, :], unit, inverse)
            input_grad_ref[rows, :] = (middle_ref[rows, :] + back).astype(BF16)
            return carry

        lax.fori_loop(0, count, one_block, 0)


def attention_back(buckets, probs, qkv, attended_low, normed, tokens, middle_grad, weight, vecs):
    rows = tokens.shape[0]
    count = rows // SLOT

    def whole(shape):
        return pl.BlockSpec(shape, lambda i: (0,) * len(shape), pipeline_mode=pl.Buffered(1))

    def held(shape):
        return pl.BlockSpec(shape, lambda i: (0,) * len(shape))

    def panel(base):
        return pl.BlockSpec((1, rows, 128), lambda i: (base + i, 0, 0))

    def weight_panel(base):
        return pl.BlockSpec((D, 128), lambda i: (0, base + i))

    return pl.pallas_call(
        attention_back_kernel,
        grid=(PAIRS,),
        in_specs=[
            pl.BlockSpec(memory_space=pltpu.SMEM),
            pl.BlockSpec((2, count, SLOT, SLOT), lambda i: (i, 0, 0, 0)),
            panel(0), panel(PAIRS), panel(2 * PAIRS),
            pl.BlockSpec((rows, 128), lambda i: (0, i)),
            whole((rows, D)), whole((rows, D)), whole((rows, D)),
            weight_panel(0), weight_panel(PAIRS), weight_panel(2 * PAIRS),
            whole((8, D)),
        ],
        out_specs=[
            held((rows, D)),
            pl.BlockSpec((2, 2, SLOT, SLOT), lambda i: (0, i, 0, 0)),
            pl.BlockSpec((1, D, 384), lambda i: (i, 0, 0)),
            pl.BlockSpec((1, 8, 384), lambda i: (i, 0, 0)),
            held((8, D)),
        ],
        out_shape=[
            jax.ShapeDtypeStruct((rows, D), BF16),
            jax.ShapeDtypeStruct((2, HEADS, SLOT, SLOT), F32),
            jax.ShapeDtypeStruct((PAIRS, D, 384), BF16),
            jax.ShapeDtypeStruct((PAIRS, 8, 384), F32),
            jax.ShapeDtypeStruct((8, D), F32),
        ],
        scratch_shapes=[
            pltpu.VMEM((D, rows), BF16),
            pltpu.VMEM((rows, D), F32),
            pltpu.VMEM((rows, 384), BF16),
        ],
        compiler_params=params(dimension_semantics=("arbitrary",)),
        name="attention_backward",
    )(buckets, probs, qkv, qkv, qkv, attended_low, normed, tokens, middle_grad, weight, weight, weight, vecs)


MESH = pl.DeviceIdType.MESH
ANY = pl.ANY


class Place:
    def __init__(self):
        fsdp = lax.axis_index("fsdp")
        dp = lax.axis_index("dp")
        self.z, self.y, self.x, self.core = fsdp // 2, fsdp % 2, dp // 2, dp % 2

    def at(self, z=None, y=None, x=None, core=None):
        z = self.z if z is None else z
        y = self.y if y is None else y
        x = self.x if x is None else x
        core = self.core if core is None else core
        return (z * 2 + y, x * 2 + core)

    def greet(self):
        barrier = pltpu.get_barrier_semaphore()
        peers = [self.at(z=(self.z + k) % 4, y=self.y) for k in range(1, 4)]
        peers += [self.at(z=(self.z + k) % 4, y=1 - self.y) for k in range(4)]
        peers += [
            self.at(x=1 - self.x),
            self.at(core=1 - self.core),
            self.at(x=1 - self.x, core=1 - self.core),
        ]
        for peer in peers:
            pl.semaphore_signal(barrier, inc=1, device_id=peer, device_id_type=MESH)
        pl.semaphore_wait(barrier, len(peers))


def remote(src, dst, send, recv, peer):
    return pltpu.make_async_remote_copy(
        src_ref=src, dst_ref=dst, send_sem=send, recv_sem=recv, device_id=peer, device_id_type=MESH
    )


def rows_of(first, size):
    return pl.ds(pl.multiple_of(first * size, size), size)


def chunk(kind, ref, r, d):
    if kind == "panel":
        return ref.at[d, rows_of(r, 96), :]
    if kind == "wide":
        return ref.at[rows_of(r, 96), rows_of(d, 768)]
    return ref.at[rows_of(d, 192), rows_of(r, 384)]


class Gather:
    def __init__(self, place, kinds, pieces, fulls, send, recv, local):
        self.place, self.kinds, self.pieces, self.fulls = place, kinds, pieces, fulls
        self.send, self.recv, self.local = send, recv, local
        self.started = []

    def slot(self, w, z, y, x, core=None):
        core = self.place.core if core is None else core
        return chunk(self.kinds[w], self.fulls[w], z * 2 + y, x * 2 + core)

    def copy(self, w, index, src, dst, peer):
        return remote(src, dst, self.send.at[w, index], self.recv.at[w, index], peer)

    def start(self, made):
        made.start()
        self.started.append(made)
        return made

    def begin(self, w):
        here = self.place
        own = self.slot(w, here.z, here.y, here.x)
        keep = pltpu.make_async_copy(self.pieces[w], own, self.local.at[w])
        keep.start()
        self.keep = getattr(self, "keep", []) + [keep]
        self.along = getattr(self, "along", {})
        for k in range(1, 4):
            peer = here.at(z=(here.z + k) % 4)
            self.along[w, k] = self.start(self.copy(w, k, self.pieces[w], own, peer))

    def source(self, w, k):
        here = self.place
        if k == 0:
            return self.pieces[w]
        return self.slot(w, (here.z + 4 - k) % 4, here.y, here.x)

    def sibling(self, w, index, src, z, y, x):
        peer = self.place.at(core=1 - self.place.core)
        self.last = getattr(self, "last", [])
        self.last.append(self.start(self.copy(w, index, src, self.slot(w, z, y, x), peer)))

    def first(self, w, k):
        here = self.place
        if k:
            self.along[w, k].wait_recv()
        z = (here.z + 4 - k) % 4
        across = 1 - z // 2
        x = here.x + across * (1 - 2 * here.x)
        y = here.y + (1 - across) * (1 - 2 * here.y)
        src = self.source(w, k)
        dst = self.slot(w, z, here.y, here.x)
        self.step = getattr(self, "step", {})
        self.step[w, k] = self.start(self.copy(w, 4 + k, src, dst, here.at(x=x, y=y)))
        self.sibling(w, 16 + 4 * k, src, z, here.y, here.x)

    def second(self, w, k):
        here = self.place
        self.step[w, k].wait_recv()
        z = (here.z + 4 - k) % 4
        across = 1 - z // 2
        near_x = here.x + across * (1 - 2 * here.x)
        near_y = here.y + (1 - across) * (1 - 2 * here.y)
        far_x = here.x + (1 - across) * (1 - 2 * here.x)
        far_y = here.y + across * (1 - 2 * here.y)
        peer = here.at(x=far_x, y=far_y)
        near = self.slot(w, z, near_y, near_x)
        self.turn = getattr(self, "turn", {})
        self.turn[w, k] = [
            self.start(self.copy(w, 8 + 2 * k, self.source(w, k), self.slot(w, z, here.y, here.x), peer)),
            self.start(self.copy(w, 9 + 2 * k, near, near, peer)),
        ]
        self.sibling(w, 17 + 4 * k, near, z, near_y, near_x)

    def third(self, w, k):
        here = self.place
        z = (here.z + 4 - k) % 4
        across = 1 - z // 2
        far_x = here.x + (1 - across) * (1 - 2 * here.x)
        far_y = here.y + across * (1 - 2 * here.y)
        for i, made in enumerate(self.turn[w, k]):
            made.wait_recv()
            if i == 0:
                x, y = far_x, far_y
            else:
                x, y = 1 - here.x, 1 - here.y
            src = self.slot(w, z, y, x)
            self.sibling(w, 18 + 4 * k + i, src, z, y, x)

    def finish(self, w):
        for made in self.last:
            made.wait_recv()
        for made in self.started:
            made.wait_send()
        for made in self.keep:
            made.wait()


GATHER_KINDS = ("panel", "panel", "wide", "turned")


def gather_kernel(
    qkv_p, out_p, up_p, down_p, vec_p, table_p, qkv_f, out_f, up_f, down_f, vec_f, table_f,
    send, recv, local, vec_send, vec_recv, vec_local,
):
    place = Place()
    place.greet()
    f = place.z * 2 + place.y
    small = []
    keep = []
    for n, (piece, full) in enumerate(((vec_p, vec_f), (table_p, table_f))):
        made = pltpu.make_async_copy(piece, full.at[f], vec_local.at[n])
        made.start()
        keep.append(made)
        for k in range(1, 8):
            peer = (f + k) % 8
            made = remote(
                piece, full.at[f], vec_send.at[n, k], vec_recv.at[n, k],
                place.at(z=peer // 2, y=peer % 2),
            )
            made.start()
            small.append(made)
    gather = Gather(
        place, GATHER_KINDS, (qkv_p, out_p, up_p, down_p), (qkv_f, out_f, up_f, down_f),
        send, recv, local,
    )
    order = [(w, k) for w in range(4) for k in range(4)]
    for w in range(4):
        gather.begin(w)
    for n in range(len(order) + 2):
        if n < len(order):
            gather.first(*order[n])
        if 0 <= n - 1 < len(order):
            gather.second(*order[n - 1])
        if 0 <= n - 2 < len(order):
            gather.third(*order[n - 2])
    gather.finish(0)
    for made in small:
        made.wait()
    for made in keep:
        made.wait()


def gather_all(qkv_p, out_p, up_p, down_p, vec_p, table_p):
    return pl.pallas_call(
        gather_kernel,
        in_specs=[pl.BlockSpec(memory_space=ANY)] * 6,
        out_specs=[pl.BlockSpec(memory_space=ANY)] * 6,
        out_shape=[
            jax.ShapeDtypeStruct((4, D, 576), BF16),
            jax.ShapeDtypeStruct((4, D, 192), BF16),
            jax.ShapeDtypeStruct((D, FF), BF16),
            jax.ShapeDtypeStruct((D, FF), BF16),
            jax.ShapeDtypeStruct((8,) + vec_p.shape, BF16),
            jax.ShapeDtypeStruct((8,) + table_p.shape, BF16),
        ],
        scratch_shapes=[
            pltpu.SemaphoreType.DMA((4, 32)),
            pltpu.SemaphoreType.DMA((4, 32)),
            pltpu.SemaphoreType.DMA((4,)),
            pltpu.SemaphoreType.DMA((2, 8)),
            pltpu.SemaphoreType.DMA((2, 8)),
            pltpu.SemaphoreType.DMA((2,)),
        ],
        compiler_params=params(collective_id=1, has_side_effects=True),
        name="gather_weights",
    )(qkv_p, out_p, up_p, down_p, vec_p, table_p)


class Scatter:
    def __init__(self, place, kind, grad, acc, from_core, half, near, far, quarter, out, sems):
        self.place, self.kind, self.grad, self.acc = place, kind, grad, acc
        self.from_core, self.half, self.near, self.far = from_core, half, near, far
        self.quarter, self.out = quarter, out
        self.send, self.recv, self.local = sems
        self.started = []

    def part(self, ref, x, r, count=1):
        if self.kind == "turned":
            return ref.at[x, :, pl.ds(pl.multiple_of(r * 384, 384), count * 384)]
        return ref.at[x, pl.ds(pl.multiple_of(r * 96, 96), count * 96), :]

    def panel(self, d):
        if self.kind == "panel":
            return self.grad.at[d]
        if self.kind == "wide":
            return self.grad.at[:, rows_of(d, 768)]
        return self.grad.at[rows_of(d, 192), :]

    def copy(self, index, src, dst, peer):
        made = remote(src, dst, self.send.at[index], self.recv.at[index], peer)
        made.start()
        self.started.append(made)
        return made

    def begin(self):
        here = self.place
        peer = here.at(core=1 - here.core)
        self.keep = []
        self.core = []
        for x in range(2):
            self.core.append(
                self.copy(x, self.panel(x * 2 + 1 - here.core), self.from_core.at[x], peer)
            )
            made = pltpu.make_async_copy(
                self.panel(x * 2 + here.core), self.acc.at[x], self.local.at[x]
            )
            made.start()
            self.keep.append(made)

    def add(self, target, source):
        if self.kind == "turned":
            size = 16
        else:
            size = 32
        rows = target.shape[0]

        def step(n, carry):
            at = pl.ds(pl.multiple_of(n * size, size), size)
            target[at, :] = target[at, :] + source[at, :]
            return carry

        lax.fori_loop(0, rows // size, step, 0)

    def plane(self):
        here = self.place
        for made in self.keep:
            made.wait()
        for made in self.core:
            made.wait_recv()
        for x in range(2):
            self.add(self.acc.at[x], self.from_core.at[x])
        over_x = here.at(x=1 - here.x)
        over_y = here.at(y=1 - here.y)
        self.wait_half = [
            self.copy(2, self.part(self.acc, 1 - here.x, 0, 4), self.half, over_x)
        ]
        for x in range(2):
            for n in range(2):
                src = self.part(self.acc, x, (2 + n) * 2 + 1 - here.y)
                self.wait_half.append(
                    self.copy(3 + 2 * x + n, src, self.near.at[x, n], over_y)
                )

    def turn(self):
        here = self.place
        for made in self.wait_half:
            made.wait_recv()
        self.add(self.part(self.acc, here.x, 0, 4), self.half)
        for x in range(2):
            for n in range(2):
                self.add(self.part(self.acc, x, (2 + n) * 2 + here.y), self.near.at[x, n])
        over_x = here.at(x=1 - here.x)
        over_y = here.at(y=1 - here.y)
        self.wait_far = []
        for n in range(2):
            src = self.part(self.acc, here.x, n * 2 + 1 - here.y)
            self.wait_far.append(self.copy(7 + n, src, self.far.at[0, n], over_y))
            src = self.part(self.acc, 1 - here.x, (2 + n) * 2 + here.y)
            self.wait_far.append(self.copy(9 + n, src, self.far.at[1, n], over_x))

    def line(self):
        here = self.place
        for made in self.wait_far:
            made.wait_recv()
        for n in range(2):
            self.add(self.part(self.acc, here.x, n * 2 + here.y), self.far.at[0, n])
            self.add(self.part(self.acc, here.x, (2 + n) * 2 + here.y), self.far.at[1, n])
        self.wait_line = []
        for k in range(1, 4):
            z = (here.z + k) % 4
            src = self.part(self.acc, here.x, z * 2 + here.y)
            self.wait_line.append(self.copy(10 + k, src, self.quarter.at[k - 1], here.at(z=z)))

    def end(self):
        here = self.place
        for made in self.wait_line:
            made.wait_recv()
        total = self.part(self.acc, here.x, here.z * 2 + here.y)[...].astype(F32)
        for k in range(3):
            total = total + self.quarter[k].astype(F32)
        self.out[...] = total
        for made in self.started:
            made.wait_send()


SCATTER_PIECES = {"qkv": (96, 576), "out": (96, 192), "up": (96, 768), "down": (192, 384)}
SCATTER_KINDS = {"qkv": "panel", "out": "panel", "up": "wide", "down": "turned"}
SCATTER_ORDER = ("down", "up", "out", "qkv")


def scatter_scratch(name):
    height, width = SCATTER_PIECES[name]
    if name == "down":
        whole, half = (2, height, 8 * width), (height, 4 * width)
    else:
        whole, half = (2, 8 * height, width), (4 * height, width)
    return [
        pltpu.VMEM(whole, BF16),
        pltpu.VMEM(whole, BF16),
        pltpu.VMEM(half, BF16),
        pltpu.VMEM((2, 2, height, width), BF16),
        pltpu.VMEM((2, 2, height, width), BF16),
        pltpu.VMEM((3, height, width), BF16),
        pltpu.SemaphoreType.DMA((14,)),
        pltpu.SemaphoreType.DMA((14,)),
        pltpu.SemaphoreType.DMA((2,)),
    ]


def pack_sums(sums_ref, first_ref, wide_ref, pair_ref, table_ref, packed):
    low = first_ref[0:2, :]
    narrow = sums_ref[...]
    group = lax.broadcasted_iota(jnp.int32, (D, 128), 0) // HEAD_DIM
    pick = (group == lax.broadcasted_iota(jnp.int32, (D, 128), 1)).astype(F32).astype(BF16)
    high, rest = split_low(narrow[8:16])
    heads = (nn(high, pick) + nn(rest, pick))[0:1]
    heads = jnp.concatenate([heads, jnp.zeros((1, 64), F32)], 1)
    query = jnp.concatenate([pair_ref[n, 0:1, 0:128] for n in range(PAIRS)], 1)
    value = jnp.concatenate([pair_ref[n, 0:1, 256:384] for n in range(PAIRS)], 1)
    pair = jnp.concatenate([query, value], 1)
    for f in range(8):
        at = slice(96 * f, 96 * f + 96)
        packed[f, 0:1, :] = jnp.concatenate(
            [low[0:1, at], low[1:2, at], narrow[2:3, at], narrow[3:4, at]], 1
        )
        packed[f, 1:2, :] = jnp.concatenate([narrow[n : n + 1, at] for n in range(4, 8)], 1)
        packed[f, 2:5, :] = wide_ref[0:3, 384 * f : 384 * f + 384]
        at = slice(192 * f, 192 * f + 192)
        packed[f, 5:6, :] = jnp.concatenate([pair[:, at], heads], 1)
        for n in range(PAIRS):
            packed[f, 6 + n : 7 + n, :] = jnp.concatenate(
                [table_ref[2 * n : 2 * n + 1, at], table_ref[2 * n + 1 : 2 * n + 2, at]], 1
            )
        packed[f, 12:16, :] = jnp.zeros((4, 384), F32)


class SmallSums:
    def __init__(self, place, packed, rows, peers, sems):
        self.place, self.packed, self.rows, self.peers = place, packed, rows, peers
        self.send, self.recv = sems

    def begin(self):
        here = self.place
        f = here.z * 2 + here.y
        self.made = []
        for k in range(1, 8):
            to = (f + k) % 8
            made = remote(
                self.packed.at[to], self.rows.at[k - 1], self.send.at[k], self.recv.at[k],
                here.at(z=to // 2, y=to % 2),
            )
            made.start()
            self.made.append(made)

    def cross(self):
        here = self.place
        f = here.z * 2 + here.y
        for made in self.made:
            made.wait()
        total = self.packed[f]
        for k in range(7):
            total = total + self.rows[k]
        self.peers[0] = total
        d = here.x * 2 + here.core
        self.made = []
        for k in range(1, 4):
            to = (d + k) % 4
            made = remote(
                self.peers.at[0], self.peers.at[k], self.send.at[7 + k], self.recv.at[7 + k],
                here.at(x=to // 2, core=to % 2),
            )
            made.start()
            self.made.append(made)

    def end(self):
        for made in self.made:
            made.wait()
        return (self.peers[0] + self.peers[1]) + (self.peers[2] + self.peers[3])


def scatter_kernel(*refs):
    grads = dict(zip(SCATTER_ORDER, refs[:4]))
    sums_ref, first_ref, wide_ref, pair_ref, table_ref = refs[4:9]
    outs = dict(zip(SCATTER_ORDER, refs[9:13]))
    small_outs = refs[13:27]
    scratch = refs[27:]
    place = Place()
    place.greet()
    parts = []
    for n, name in enumerate(SCATTER_ORDER):
        own = scratch[9 * n : 9 * n + 9]
        parts.append(
            Scatter(
                place, SCATTER_KINDS[name], grads[name], *own[:6], outs[name], own[6:]
            )
        )
    packed, rows, peers, send, recv = scratch[36:]
    small = SmallSums(place, packed, rows, peers, (send, recv))
    for part in parts:
        part.begin()
    pack_sums(sums_ref, first_ref, wide_ref, pair_ref, table_ref, packed)
    small.begin()
    for n in range(len(parts) + 3):
        if n < len(parts):
            parts[n].plane()
        if 0 <= n - 1 < len(parts):
            parts[n - 1].turn()
        if 0 <= n - 2 < len(parts):
            parts[n - 2].line()
        if n == 2:
            small.cross()
        if 0 <= n - 3 < len(parts):
            parts[n - 3].end()
    total = small.end()
    for n in range(8):
        small_outs[n][...] = total[n // 4 : n // 4 + 1, 96 * (n % 4) : 96 * (n % 4) + 96]
    for n in range(3):
        small_outs[8 + n][...] = total[2 + n : 3 + n, :]
    small_outs[11][...] = total[5:6, 0:192]
    small_outs[12][...] = total[5:6, 192:204]
    small_outs[13][...] = jnp.concatenate(
        [total[6:12, 0:192], total[6:12, 192:384], jnp.zeros((4, 192), F32)], 0
    )


def scatter_all(down, up, out, qkv, sums, first, wide, pair, table):
    vmem = pl.BlockSpec(memory_space=pltpu.VMEM)
    scratch = []
    for name in SCATTER_ORDER:
        scratch += scatter_scratch(name)
    small = [(1, 96)] * 8 + [(1, 384)] * 3 + [(1, 192), (1, 12), (16, 192)]
    shapes = [SCATTER_PIECES[name] for name in SCATTER_ORDER] + small
    return pl.pallas_call(
        scatter_kernel,
        in_specs=[pl.BlockSpec(memory_space=ANY)] * 4 + [vmem] * 5,
        out_specs=[vmem] * len(shapes),
        out_shape=[jax.ShapeDtypeStruct(shape, F32) for shape in shapes],
        scratch_shapes=scratch
        + [
            pltpu.VMEM((8, 16, 384), F32),
            pltpu.VMEM((7, 16, 384), F32),
            pltpu.VMEM((4, 16, 384), F32),
            pltpu.SemaphoreType.DMA((11,)),
            pltpu.SemaphoreType.DMA((11,)),
        ],
        compiler_params=params(collective_id=2, has_side_effects=True),
        name="scatter_grads",
    )(down, up, out, qkv, sums, first, wide, pair, table)


def gather_matrix(piece):
    rows = lax.all_gather(piece, "fsdp", axis=0, tiled=True)
    return lax.all_gather(rows, "dp", axis=1, tiled=True)


def scatter_matrix(grad):
    part = lax.psum_scatter(grad, "dp", scatter_dimension=1, tiled=True).astype(F32)
    return lax.psum_scatter(part, "fsdp", scatter_dimension=0, tiled=True)


def body(
    tokens, cotangent, lengths, buckets, qkv_weight, query_value_bias, out_weight, out_bias,
    up_weight, up_bias, down_weight, down_bias, first_gain, first_shift, mix_gain, mix_shift,
    second_gain, second_shift, hidden_gain, hidden_shift, head_scale, position_table,
):
    parts = lax.axis_size("fsdp")
    own_kernels = (parts, lax.axis_size("dp")) == (8, 4)
    narrow = [
        first_gain, first_shift, mix_gain, mix_shift, second_gain, second_shift, out_bias, down_bias,
    ]
    wide = [up_bias, hidden_gain, hidden_shift]
    a = D // parts
    b = FF // parts
    packed = jnp.concatenate(
        [jnp.pad(jnp.stack(narrow), ((0, 0), (0, b - a))), jnp.stack(wide)]
        + [jnp.pad(query_value_bias, (0, b - 2 * a))[None], jnp.zeros((4, b), BF16)]
    )
    if own_kernels:
        qkv_full, out_full, up_full, down_full, gathered, table = gather_all(
            qkv_weight, out_weight, up_weight, down_weight.T, packed, position_table
        )
        qkv_full = qkv_full.transpose(1, 0, 2).reshape(D, 3 * D)
        out_full = out_full.transpose(1, 0, 2).reshape(D, D)
    else:
        gathered = lax.all_gather(packed, "fsdp", axis=0)
        table = lax.all_gather(position_table, "fsdp", axis=0)
        qkv_full = gather_matrix(qkv_weight)
        out_full = gather_matrix(out_weight)
        up_full = gather_matrix(up_weight)
        down_full = gather_matrix(down_weight).T
    gathered = gathered.astype(F32)
    vecs = gathered[:, :8, :a].transpose(1, 0, 2).reshape(8, D)
    wides = jnp.pad(gathered[:, 8:11].transpose(1, 0, 2).reshape(3, FF), ((0, 5), (0, 0)))
    pair = gathered[:, 11, : 2 * a].reshape(1, 2 * D)
    table = jnp.pad(table.astype(F32).reshape(TABLE, HEADS).T, ((0, 4), (0, 0)))
    qkv_bias = jnp.concatenate([pair[:, :D], jnp.zeros((1, D), F32), pair[:, D:]], 1)
    scales = jnp.repeat(head_scale.astype(F32), HEAD_DIM)[None]

    bias = build_bias(table)
    normed, qkv, probs, attended = attention(
        lengths, buckets, tokens, vecs, qkv_full, qkv_bias, bias
    )
    (
        result, mixed, second, act, low, branch, middle_grad, attended_low, sums, wide_sums,
    ) = feed_forward(tokens, attended, cotangent, out_full, up_full, down_full, vecs, wides, scales)
    down_grad = outer_product(cotangent, act, 512)
    up_grad = outer_product(second, low, 512)
    out_grad = outer_product(mixed, branch, 256)
    input_grad, grids, qkv_grad, pair_sums, first_sums = attention_back(
        buckets, probs, qkv, attended_low, normed, tokens, middle_grad, qkv_full, vecs
    )
    table_sums = table_grad(grids)
    qkv_natural = qkv_grad.reshape(PAIRS, D, 3, 128).transpose(1, 2, 0, 3).reshape(D, 3 * D)

    if own_kernels:
        owned = scatter_all(
            down_grad, up_grad, out_grad.reshape(D, 4, 192).transpose(1, 0, 2),
            qkv_natural.reshape(D, 4, 576).transpose(1, 0, 2),
            sums, first_sums, wide_sums, pair_sums, table_sums,
        )
        down_owned, up_owned, out_owned, qkv_owned = owned[0].T, owned[1], owned[2], owned[3]
        narrow_owned = [part.reshape(-1) for part in owned[4:12]]
        wide_owned = [part.reshape(-1) for part in owned[12:15]]
        pair_owned = owned[15].reshape(-1)
        scale_grad = owned[16].reshape(-1)
        table_owned = owned[17][:HEADS].reshape(2, PAIRS, -1).transpose(2, 1, 0).reshape(-1, HEADS)
    else:
        qkv_owned = scatter_matrix(qkv_natural)
        out_owned = scatter_matrix(out_grad)
        up_owned = scatter_matrix(up_grad)
        down_owned = scatter_matrix(down_grad.T)
        pair_grad = pair_sums[:, 0].reshape(PAIRS, 3, 128).transpose(1, 0, 2).reshape(3, D)
        pair_grad = jnp.concatenate([pair_grad[0], pair_grad[2]])
        narrow_sums = jnp.concatenate([first_sums[:2], sums[2:8]], 0)
        packed = jnp.concatenate(
            [
                narrow_sums.reshape(8, parts, a).transpose(1, 0, 2).reshape(parts, -1),
                wide_sums[:3].reshape(3, parts, b).transpose(1, 0, 2).reshape(parts, -1),
                pair_grad.reshape(parts, -1),
                table_sums[:HEADS].T.reshape(parts, -1),
            ],
            1,
        )
        owned = lax.psum(lax.psum_scatter(packed, "fsdp", scatter_dimension=0, tiled=True), "dp")[0]
        scale_grad = lax.psum(sums[8].reshape(HEADS, HEAD_DIM).sum(1), ("fsdp", "dp"))
        narrow_owned = owned[: 8 * a].reshape(8, a)
        edge = 8 * a
        wide_owned = owned[edge : edge + 3 * b].reshape(3, b)
        edge += 3 * b
        pair_owned = owned[edge : edge + 2 * a]
        edge += 2 * a
        table_owned = owned[edge:].reshape(TABLE // parts, HEADS)
    return (
        result, input_grad, qkv_owned, pair_owned, out_owned, narrow_owned[6], up_owned,
        wide_owned[0], down_owned, narrow_owned[7], narrow_owned[0], narrow_owned[1],
        narrow_owned[2], narrow_owned[3], narrow_owned[4], narrow_owned[5], wide_owned[1],
        wide_owned[2], scale_grad, table_owned,
    )


def solution(mesh):
    tokens = P(("fsdp", "dp"), None)
    sequences = P(("fsdp", "dp"))
    matrix = P("fsdp", "dp")
    vector = P("fsdp")
    table = P("fsdp", None)
    in_specs = (
        tokens, tokens, sequences, sequences, matrix, vector, matrix, vector, matrix, vector,
        matrix, vector, vector, vector, vector, vector, vector, vector, vector, vector, P(), table,
    )
    out_specs = (
        tokens, tokens, matrix, vector, matrix, vector, matrix, vector, matrix, vector, vector,
        vector, vector, vector, vector, vector, vector, vector, P(), table,
    )
    return jax.shard_map(body, mesh=mesh, in_specs=in_specs, out_specs=out_specs, check_vma=False)
```

time: 1380 us -> 420 us (0.30)
  local copies, waits for them, and re-layouts: 482 us -> 57.6 us
  Pallas kernels: 0 us -> 355 us
  waiting for transfers between devices: 330 us -> 0 us
  blocking collectives: 263 us -> 0 us
  matrix products: 171 us -> 0 us
  other arithmetic: 106 us -> 5.92 us
  between operations: 19.1 us -> 0.77 us
    pallas_call x0 -> x10, Pallas kernels: none -> 355 us  [the longest x1 114 us: gather_all(): pl.pallas_call(gather_kernel, in_specs=[pl.BlockSpec(memory_space=ANY)] *...]
    reshape x31 -> x7, local copies, waits for them, and re-layouts: 209 us -> 10.3 us  [the longest x1 4.08 us: body(): qkv_full = qkv_full.transpose(1, 0, 2).reshape(D, 3 * D)]
    unnamed x20 -> x0, waiting for transfers between devices: 185 us -> none
    all_gather x6 -> x0, blocking collectives: 175 us -> none  [the longest x1 35.7 us: gather_weights(): lax.all_gather(pieces[0], 'fsdp', axis=0, tiled=True)]
    dot_general x20 -> x0, matrix products: 171 us -> none  [the longest x1 39.4 us: forward_pass(): jnp.dot(second, up_weight, preferred_element_type=jnp.float32)]
    reduce_scatter x6 -> x0, waiting for transfers between devices: 145 us -> none  [the longest x1 72.5 us: scatter_grads(): lax.psum_scatter(cols[3], 'fsdp', scatter_dimension=0, tiled=True)]
    reduce_sum x22 -> x0, other arithmetic: 78 us -> none  [the longest x6 24.5 us: toeplitz(): tiled = jnp.tile(line, (1,) * (line.ndim - 1) + (count + 1,))]
    pad x14 -> x3, local copies, waits for them, and re-layouts: 52.7 us -> 1.32 us  [the longest x1 0.66 us: body(): jnp.pad(query_value_bias, (0, b - 2 * a))[None]]
  transfers between devices with their start and end apart: 16 -> 0, of which waited for: 6 -> 0; matrix products, arithmetic and copies ran while one was open for 47% -> 0% of each run, Pallas kernels for 0% -> 0%
where the time goes in v1:
time: 420 us; the launch traced here: 419 us
  Pallas kernels  355 us (85%)
  local copies, waits for them, and re-layouts  57.6 us (14%)
  other arithmetic  5.92 us (1%)
    pallas_call x1, Pallas kernels, gather_all(): pl.pallas_call(gather_kernel, in_specs=[pl.BlockSpec(memory_space=ANY)] *...  114 us
    pallas_call x1, Pallas kernels, scatter_all(): pl.pallas_call(scatter_kernel, in_specs=[pl.BlockSpec(memory_space=ANY)]...  87.6 us
    pallas_call x1, Pallas kernels, feed_forward(): pl.pallas_call(feed_kernel, grid=(rows // tile,), in_specs=[block] * 3 +...  47.4 us
    pallas_call x1, Pallas kernels, attention_back(): pl.pallas_call(attention_back_kernel, grid=(PAIRS,), in_specs=[pl.BlockSp...  36.6 us
    pallas_call x1, Pallas kernels, attention(): pl.pallas_call(attention_kernel, in_specs=[smem, smem] + [vmem] * 5, out_...  28.2 us
    pallas_call x3, Pallas kernels, outer_product(): pl.pallas_call(outer_kernel, grid=(cols // panel,), in_specs=[pl.BlockSpe...  25.9 us
    unnamed x15, local copies, waits for them, and re-layouts  19.7 us
    pallas_call x1, Pallas kernels, table_grad(): pl.pallas_call(table_grad_kernel, out_shape=jax.ShapeDtypeStruct((16, TAB...  8.89 us

profile of v1, /device:TPU:0, one launch (start us, length us, event | category | flops | bytes accessed | tf_op | source)
XLA Modules:
  0.0 419.0 jit_solution(15860205071078649247)
XLA Ops:
  4.2 1.2 concatenate.6.vec_p
  6.8 1.4 copy.63.table_p
  8.2 114.3 %gather_weights.1 = (bf16[4,768,576]{2,1,0:T(8,128)(2,1)}, bf16[4,768,192]{2,1,0:T(8,128)(2,1)}, bf16[768,3072]{1,0:T(8,128)(2,1)}, bf16[768,3072]{1,0:T(8,128)(...) custom-call(bf16[96,576]{1,0:T(8,128)(2,1)} %qkv_p.1, bf16[96,192]{1,0:T(8,128)(2,1)} %out_p.1, ...), custom_call_target="tpu_custom_call" | custom-call | tf_op jit(solution)/shard_map/gather_weights/pallas_call | solution.py:723
  122.5 4.4 %copy.65 = bf16[768,4,576]{0,2,1:T(8,128)(2,1)S(1)} copy(bf16[768,4,576]{2,0,1:T(8,128)(2,1)} %bitcast.49) | data formatting | bytes 7077888 | tf_op jit(solution)/shard_map/transpose | solution.py:1061
  127.0 4.1 copy.67.weight_ref.weight_q.weight_k.weight_v
  136.7 1.7 copy.68
  138.4 1.5 copy.69.out_w
  139.8 5.9 %build_bias.1.bias_ref = bf16[2,12,256,256]{3,2,1,0:T(8,128)(2,1)} custom-call(f32[16,1536]{1,0:T(8,128)} %pad_convert_fusion.table_ref), custom_call_target="tpu_custom_call" | custom-call | tf_op jit(solution)/shard_map/build_bias/pallas_call | solution.py:118
  145.7 28.2 %attention_forward.1 = (bf16[1024,768]{1,0:T(8,128)(2,1)}, bf16[18,1024,128]{2,1,0:T(8,128)(2,1)}, bf16[12,4,256,256]{3,2,1,0:T(8,128)(2,1)}, f32[1024,768]{1,0:T(8,128)}) custom-call(s32[4]{0:T(128)} %lengths.1, s32[4]{0:T(128)} %buckets.3, bf16[1024,768]{1,0:T(8,128)(2,1)} %x_ref.5, f32[8,768]{1,0:T(8,128)} %reshape.107.vec_ref, ...), custom_call_target="tpu_custom_call" | custom-call | tf_op jit(solution)/shard_map/attention_forward/pallas_call | solution.py:245
  173.9 47.4 %feed_forward.1 = (bf16[1024,768]{1,0:T(8,128)(2,1)}, bf16[1024,768]{1,0:T(8,128)(2,1)}, bf16[1024,768]{1,0:T(8,128)(2,1)}, bf16[1024,3072]{1,0:T(8,128)(2,1)}, ...) custom-call(bf16[1024,768]{1,0:T(8,128)(2,1)} %x_ref.5, ...), custom_call_target="tpu_custom_call" | custom-call | tf_op jit(solution)/shard_map/feed_forward/pallas_call | solution.py:357
  221.3 36.6 %attention_backward.1 = (bf16[1024,768]{1,0:T(8,128)(2,1)}, f32[2,12,256,256]{3,2,1,0:T(8,128)}, bf16[6,768,384]{2,1,0:T(8,128)(2,1)}, f32[6,8,384]{2,1,0:T(8,128)}, f32[8,768]{1,0:T(8,128)}) custom-call(s32[4]{0:T(128)} %buckets.3, bf16[12,4,256,256]{3,2,1,0:T(8,128)(2,1)} %get-tuple-element.71.probs_ref, ...), custom_call_target="tpu_custom_call" | custom-call | tf_op jit(solution)/shard_map/attention_backward/pallas_call | solution.py:496
  257.9 8.9 %table_grad.1.refs_8_ = f32[16,1536]{1,0:T(8,128)} custom-call(f32[2,12,256,256]{3,2,1,0:T(8,128)} %get-tuple-element.87.grid_ref), custom_call_target="tpu_custom_call" | custom-call | tf_op jit(solution)/shard_map/table_grad/pallas_call | solution.py:181
  266.8 5.2 %weight_grad.5 = bf16[768,768]{1,0:T(8,128)(2,1)} custom-call(bf16[1024,768]{1,0:T(8,128)(2,1)} %get-tuple-element.80.left_ref, bf16[1024,768]{1,0:T(8,128)(2,1)} %get-tuple-element.81.right_ref), custom_call_target="tpu_custom_call" | custom-call | tf_op jit(solution)/shard_map/weight_grad/pallas_call | solution.py:393
  272.0 1.6 copy.73
  273.6 1.6 copy.74
  275.1 6.0 %copy.75 = bf16[6,768,384]{1,2,0:T(8,128)(2,1)} copy(bf16[6,768,384]{2,1,0:T(8,128)(2,1)} %get-tuple-element.82) | data formatting | bytes 7077888 | tf_op jit(solution)/shard_map/attention_backward/pallas_call | solution.py:496
  281.1 2.2 copy.76
  283.4 3.9 copy.77
  287.3 10.3 %weight_grad.3.refs_0_ = bf16[768,3072]{1,0:T(8,128)(2,1)} custom-call(bf16[1024,768]{1,0:T(8,128)(2,1)} %left_ref.1, bf16[1024,3072]{1,0:T(8,128)(2,1)} %get-tuple-element.77.right_ref), custom_call_target="tpu_custom_call" | custom-call | tf_op jit(solution)/shard_map/weight_grad/pallas_call | solution.py:393
  297.6 10.4 %weight_grad.4.refs_1_ = bf16[768,3072]{1,0:T(8,128)(2,1)} custom-call(bf16[1024,768]{1,0:T(8,128)(2,1)} %get-tuple-element.78.left_ref, bf16[1024,3072]{1,0:T(8,128)(2,1)} %get-tuple-element.79.right_ref), custom_call_target="tpu_custom_call" | custom-call | tf_op jit(solution)/shard_map/weight_grad/pallas_call | solution.py:393
  308.0 87.6 %scatter_grads.1 = (f32[192,384]{1,0:T(8,128)}, f32[96,768]{1,0:T(8,128)}, f32[96,192]{1,0:T(8,128)}, f32[96,576]{1,0:T(8,128)}, f32[1,96]{1,0:T(1,128)}, /*inde...) custom-call(bf16[768,3072]{1,0:T(8,128)(2,1)} %weight_grad.3.refs_0_, ...), custom_call_target="tpu_custom_call" | custom-call | tf_op jit(solution)/shard_map/scatter_grads/pallas_call | solution.py:1012
  395.7 1.3 reduce.1
  396.9 1.3 reduce.2
  398.2 1.2 reduce.3
  400.8 1.7 copy.94
  402.4 1.2 copy.95
  403.6 1.5 copy.96
  406.3 1.7 copy.98
  408.0 1.7 copy.99
  410.8 1.2 copy.101
  415.5 1.2 copy.105
  417.9 1.2 copy.107
  (33 shorter events, 18.8 us)
